TPU v7x, 32 devices: a whole 2x2x4 slice. The times are simulated.
32 devices in a mesh: dp: 8 (over z, x), ctx: 4 (over y, core).
Axes of the slice: x: 2, y: 2, z: 4, core: 2. Of those that a mesh axis runs over, the one named last changes fastest.
Arguments:
- tokens: bfloat16 [16, 2048, 768], P('dp', 'ctx'), may hold values from -6 to 6
- cotangent: bfloat16 [16, 2048, 768], P('dp', 'ctx'), may hold values from -6 to 6
- lengths: int32 [16], P('dp'), may hold values from 1 to 2048, as said below
- adapter_ids: int32 [16], P('dp'), may hold values from 0 to 7
- norm_gain: float32 [768], replicated, may hold values from 0.5 to 1.5
- w_in: bfloat16 [768, 3352], P('dp'), may hold values from -0.21875 to 0.21875
- conv_weight: float32 [4, 1792], replicated, may hold values from -3 to 3
- conv_bias: float32 [1792], replicated, may hold values from -1.5 to 1.5
- dt_bias: float32 [24], replicated, may hold values from -7 to -2
- a_log: float32 [24], replicated, may hold values from 0 to 1.5
- skip_scale: float32 [24], replicated, may hold values from 0.5 to 1.5
- inner_gain: float32 [1536], replicated, may hold values from 0.5 to 1.5
- w_out: bfloat16 [1536, 768], P('dp'), may hold values from -0.15625 to 0.15625
- in_a: bfloat16 [8, 768, 16], replicated, may hold values from -0.21875 to 0.21875
- in_b: bfloat16 [8, 16, 3072], replicated, may hold values from -1.5 to 1.5
- out_a: bfloat16 [8, 1536, 16], replicated, may hold values from -0.15625 to 0.15625
- out_b: bfloat16 [8, 16, 768], replicated, may hold values from -1.5 to 1.5
Outputs:
- output: bfloat16 [16, 2048, 768], P('dp', 'ctx')
- input_grad: float32 [16, 2048, 768], P('dp', 'ctx')
- grad_in_a: float32 [8, 768, 16], P(None, 'dp')
- grad_in_b: float32 [8, 16, 3072], P(None, None, 'dp')
- grad_out_a: float32 [8, 1536, 16], P(None, 'dp')
- grad_out_b: float32 [8, 16, 768], P(None, None, 'dp')
Inputs may be any that keep to these rules, and one draw needn't show every extreme that they name: `lengths`: in each aligned group of 2 sequences (those of one index of dp) one sequence, drawn from the seed, has length 2048; the others at least 512.
All inputs are finite; a program needn't handle non-finite values.
Results may differ from a plain program's by a relative error of at most 0.0081.
Values may be sent and summed in bfloat16 or wider, within the bound.
No kernel may reach another device: no remote copies, remote signals or barrier semaphores. Data moves between devices by JAX's collectives and lax.ppermute only.
A program may use at most 256 MiB of HBM per device.

v0:
```python
import jax
import jax.numpy as jnp
from jax import lax
from jax.sharding import PartitionSpec as P

HEADS = 24
HDIM = 64
NSTATE = 128
INNER = 1536
BLOCK = 256
CONV_CH = 1792
ZX = 3072


epsilon = 1e-05
precise = lax.Precision.HIGHEST


def passed_along(value, axis, steps):
    count = lax.axis_size(axis)
    leading, last = (max(0, -steps), min(count, count - steps))
    return lax.ppermute(value, axis, [(source, source + steps) for source in range(leading, last)])


def prefix(shard, axis, join, neutral):
    place = lax.axis_index(axis)
    gathered = jax.tree.map(
        lambda a, kind: lax.all_gather(a.astype(kind), axis), shard, (jnp.bfloat16, jnp.bfloat16)
    )
    state = jax.tree.map(lambda a, e: jnp.zeros_like(a) + jnp.asarray(e, a.dtype), shard, neutral)

    def prefix_one(turn, state):
        return join(
            state,
            jax.tree.map(
                lambda a, own: lax.dynamic_index_in_dim(a, turn, 0, False).astype(own.dtype),
                gathered,
                shard,
            ),
        )

    return lax.fori_loop(0, place, prefix_one, state)


def carried_in(shard, axis, join, neutral):
    count = lax.axis_size(axis)
    place = lax.axis_index(axis)
    ahead = count - 1 - place
    gathered = jax.tree.map(
        lambda a, kind: lax.all_gather(a.astype(kind), axis),
        shard,
        jax.tree.map(lambda a: jnp.bfloat16 if a.dtype == jnp.float32 else a.dtype, shard),
    )
    state = jax.tree.map(lambda a, e: jnp.zeros_like(a) + jnp.asarray(e, a.dtype), shard, neutral)

    def carried_one(turn, state):
        source = count - 1 - turn
        return join(
            state,
            jax.tree.map(
                lambda a, own: lax.dynamic_index_in_dim(a, source, 0, False).astype(own.dtype),
                gathered,
                shard,
            ),
        )

    return lax.fori_loop(0, ahead, carried_one, state)


def matmul(left, right):
    return jnp.dot(left, right, preferred_element_type=jnp.float32)


def contract_rows(left, right):
    return lax.dot_general(
        left, right, (((0,), (0,)), ((), ())), preferred_element_type=jnp.float32
    )


def contract_cols(left, right):
    return lax.dot_general(
        left, right, (((1,), (1,)), ((), ())), preferred_element_type=jnp.float32
    )


def choose_table(selector, table):
    return jnp.einsum("a,abc->bc", selector, table, preferred_element_type=jnp.float32).astype(
        jnp.bfloat16
    )


def link_states(earlier, later):
    return (earlier[0] * later[0], later[0][:, None, None] * earlier[1] + later[1])


def conv_silu(extended, conv_weight, conv_bias):
    length_out = extended.shape[0] - conv_weight.shape[0] + 1
    summed = conv_bias[None, :] + conv_weight[0][None, :] * extended[:length_out]
    for offset in range(1, conv_weight.shape[0]):
        summed = summed + conv_weight[offset][None, :] * extended[offset : offset + length_out]
    return jax.nn.silu(summed)


def block_logs(step_dt, a_rate):
    blocks = step_dt.shape[0] // BLOCK
    return jnp.cumsum((step_dt * a_rate[None, :]).reshape(blocks, BLOCK, HEADS), axis=1)


def block_terms(ssm_x, coef_b, step_dt, a_rate):
    blocks = ssm_x.shape[0] // BLOCK
    cum_log = block_logs(step_dt, a_rate)
    to_end = jnp.exp(cum_log[:, -1:, :] - cum_log) * step_dt.reshape(blocks, BLOCK, HEADS)
    states = jnp.einsum(
        "cqh,cqn,cqhp->chpn",
        to_end,
        coef_b.reshape(blocks, BLOCK, NSTATE),
        ssm_x.reshape(blocks, BLOCK, HEADS, HDIM),
        precision=precise,
    )
    return (states, jnp.exp(cum_log[:, -1, :]))


def fold_blocks(states, totals):

    def absorb(carried, block_item):
        return (
            (carried[0] * block_item[1], block_item[1][:, None, None] * carried[1] + block_item[0]),
            None,
        )

    start = (jnp.ones((HEADS,), jnp.float32), jnp.zeros((HEADS, HDIM, NSTATE), jnp.float32))
    folded, _ = lax.scan(absorb, start, (states, totals))
    return folded


def block_outputs(ssm_x, coef_b, coef_c, step_dt, a_rate, states, totals, h_in):
    blocks = ssm_x.shape[0] // BLOCK

    def advance(carried, block_item):
        return (block_item[1][:, None, None] * carried + block_item[0], carried)

    _, incoming = lax.scan(advance, h_in, (states, totals))
    cum_log = block_logs(step_dt, a_rate)
    b_blocks = coef_b.reshape(blocks, BLOCK, NSTATE)
    c_blocks = coef_c.reshape(blocks, BLOCK, NSTATE)
    x_blocks = (ssm_x * step_dt[:, :, None]).reshape(blocks, BLOCK, HEADS, HDIM)
    scores = jnp.einsum("cqn,csn->cqs", c_blocks, b_blocks, precision=precise)
    log_heads = jnp.transpose(cum_log, (0, 2, 1))
    gaps = log_heads[:, :, :, None] - log_heads[:, :, None, :]
    causal = jnp.arange(BLOCK)[:, None] >= jnp.arange(BLOCK)[None, :]
    weights = jnp.exp(jnp.where(causal, gaps, -1e30)) * scores[:, None]
    inside = jnp.einsum("chqs,cshp->cqhp", weights, x_blocks, precision=precise)
    from_state = jnp.einsum("cqn,chpn->cqhp", c_blocks, incoming, precision=precise)
    from_state = from_state * jnp.exp(cum_log)[:, :, :, None]
    return (inside + from_state).reshape(ssm_x.shape[0], HEADS * HDIM)


def mixer_tail(y_ssm, ssm_x, gate_in, skip_scale, inner_gain):
    with_skip = y_ssm + (ssm_x * skip_scale[None, :, None]).reshape(y_ssm.shape)
    gated = with_skip * jax.nn.silu(gate_in)
    return gated * lax.rsqrt(jnp.mean(gated * gated, -1, keepdims=True) + epsilon) * inner_gain


def shards(
    tokens,
    cotangent,
    lengths,
    adapter_ids,
    norm_gain,
    w_in,
    conv_weight,
    conv_bias,
    dt_bias,
    a_log,
    skip_scale,
    inner_gain,
    w_out,
    in_a,
    in_b,
    out_a,
    out_b,
):
    slots = tokens.shape[1]
    rim_rows = conv_weight.shape[0] - 1
    positions = lax.axis_index("ctx") * slots + jnp.arange(slots, dtype=jnp.int32)
    a_rate = -jnp.exp(a_log)
    gradients = [
        jnp.zeros(in_a.shape, jnp.float32),
        jnp.zeros(in_b.shape, jnp.float32),
        jnp.zeros(out_a.shape, jnp.float32),
        jnp.zeros(out_b.shape, jnp.float32),
    ]
    outputs = []
    input_grads = []

    def norm_input(x_rows):
        return (
            x_rows * lax.rsqrt(jnp.mean(x_rows * x_rows, -1, keepdims=True) + epsilon) * norm_gain
        )

    def front(extended, dt_raw):
        activated = conv_silu(extended, conv_weight, conv_bias)
        ssm_x = activated[:, :INNER].reshape(-1, HEADS, HDIM)
        coef_b = activated[:, INNER : INNER + NSTATE]
        coef_c = activated[:, INNER + NSTATE :]
        step_dt = jax.nn.softplus(dt_raw + dt_bias[None, :])
        return (ssm_x, coef_b, coef_c, step_dt)

    def block_local(ssm_x, coef_b, step_dt):
        return block_terms(ssm_x, coef_b, step_dt, a_rate)

    def tail(ssm_x, coef_b, coef_c, step_dt, states, totals, h_in, gate_in):
        y_ssm = block_outputs(ssm_x, coef_b, coef_c, step_dt, a_rate, states, totals, h_in)
        return mixer_tail(y_ssm, ssm_x, gate_in, skip_scale, inner_gain)

    for batch_index in range(tokens.shape[0]):
        full_in, full_out = (
            lax.all_gather(w_in, "dp", axis=0, tiled=True),
            lax.all_gather(w_out, "dp", axis=0, tiled=True),
        )
        x_rows = tokens[batch_index].astype(jnp.float32)
        valid = (positions < lengths[batch_index]).astype(jnp.float32)[:, None]
        selector = (jnp.arange(in_a.shape[0], dtype=jnp.int32) == adapter_ids[batch_index]).astype(
            jnp.float32
        )
        sel_low = selector.astype(jnp.bfloat16)
        a_in = choose_table(sel_low, in_a)
        b_in = choose_table(sel_low, in_b)
        a_out = choose_table(sel_low, out_a)
        b_out = choose_table(sel_low, out_b)
        normed, norm_back = jax.vjp(norm_input, x_rows)
        normed_low = normed.astype(jnp.bfloat16)
        latent_low = matmul(normed_low, a_in).astype(jnp.bfloat16)
        projected = matmul(normed_low, full_in)
        projected = jnp.concatenate(
            [projected[:, :ZX] + matmul(latent_low, b_in), projected[:, ZX:]], axis=1
        )
        gate_in = projected[:, :INNER]
        xbc_low = projected[:, INNER : INNER + CONV_CH].astype(jnp.bfloat16)
        dt_raw = projected[:, INNER + CONV_CH :]
        rim_in = passed_along(xbc_low[slots - rim_rows :], "ctx", 1)
        extended = jnp.concatenate([rim_in, xbc_low], axis=0).astype(jnp.float32)
        (ssm_x, coef_b, coef_c, step_dt), front_back = jax.vjp(front, extended, dt_raw)
        (states, totals), block_back = jax.vjp(block_local, ssm_x, coef_b, step_dt)
        (decay, carried), fold_back = jax.vjp(fold_blocks, states, totals)
        identity = (jnp.ones_like(decay), jnp.zeros_like(carried))
        decay_in, h_in = prefix((decay, carried), "ctx", link_states, identity)
        hidden, tail_back = jax.vjp(
            tail, ssm_x, coef_b, coef_c, step_dt, states, totals, h_in, gate_in
        )
        hidden_low = hidden.astype(jnp.bfloat16)
        latent_out = matmul(hidden_low, a_out).astype(jnp.bfloat16)
        mixed = matmul(hidden_low, full_out) + matmul(latent_out, b_out)
        outputs.append((valid * (x_rows + mixed)).astype(jnp.bfloat16))
        back_in, back_out = (
            lax.all_gather(w_in, "dp", axis=0, tiled=True),
            lax.all_gather(w_out, "dp", axis=0, tiled=True),
        )
        grad_low = cotangent[batch_index] * valid.astype(jnp.bfloat16)
        d_latent_out = contract_cols(grad_low, b_out).astype(jnp.bfloat16)
        d_hidden = contract_cols(grad_low, back_out) + contract_cols(d_latent_out, a_out)
        term_out_b = contract_rows(latent_out, grad_low)
        term_out_a = contract_rows(hidden_low, d_latent_out)
        d_ssm_x, d_coef_b, d_coef_c, d_step, d_states, d_totals, d_h_in, d_gate = tail_back(
            d_hidden
        )
        decay_after, d_after = carried_in((decay, d_h_in), "ctx", link_states, identity)
        d_decay = jnp.sum(d_after * h_in, axis=(1, 2))
        d_states_fold, d_totals_fold = fold_back((d_decay, d_after))
        d_ssm_more, d_coef_more, d_step_more = block_back(
            (d_states + d_states_fold, d_totals + d_totals_fold)
        )
        d_extended, d_raw = front_back(
            (d_ssm_x + d_ssm_more, d_coef_b + d_coef_more, d_coef_c, d_step + d_step_more)
        )
        d_rim = passed_along(d_extended[:rim_rows], "ctx", -1)
        d_xbc = d_extended[rim_rows:] + jnp.pad(d_rim, ((slots - rim_rows, 0), (0, 0)))
        d_proj = jnp.concatenate([d_gate, d_xbc, d_raw], axis=1).astype(jnp.bfloat16)
        d_latent = contract_cols(d_proj[:, :ZX], b_in).astype(jnp.bfloat16)
        d_normed = contract_cols(d_proj, back_in) + contract_cols(d_latent, a_in)
        term_in_b = contract_rows(latent_low, d_proj[:, :ZX])
        term_in_a = contract_rows(normed_low, d_latent)
        (d_rows,) = norm_back(d_normed)
        input_grads.append(d_rows + valid * cotangent[batch_index].astype(jnp.float32))
        gradients = [
            gradients[0] + selector[:, None, None] * term_in_a[None],
            gradients[1] + selector[:, None, None] * term_in_b[None],
            gradients[2] + selector[:, None, None] * term_out_a[None],
            gradients[3] + selector[:, None, None] * term_out_b[None],
        ]
    summed = lax.psum((gradients[0], gradients[1], gradients[2], gradients[3]), "ctx")
    shares = (
        lax.psum_scatter(summed[0], "dp", scatter_dimension=1, tiled=True),
        lax.psum_scatter(summed[1], "dp", scatter_dimension=2, tiled=True),
        lax.psum_scatter(summed[2], "dp", scatter_dimension=1, tiled=True),
        lax.psum_scatter(summed[3], "dp", scatter_dimension=2, tiled=True),
    )
    return (jnp.stack(outputs), jnp.stack(input_grads), shares[0], shares[1], shares[2], shares[3])


def solution(mesh):
    return jax.shard_map(
        shards,
        mesh=mesh,
        in_specs=(
            P("dp", "ctx", None),
            P("dp", "ctx", None),
            P("dp"),
            P("dp"),
            P(),
            P("dp", None),
            P(),
            P(),
            P(),
            P(),
            P(),
            P(),
            P("dp", None),
            P(),
            P(),
            P(),
            P(),
        ),
        out_specs=(
            P("dp", "ctx", None),
            P("dp", "ctx", None),
            P(None, "dp", None),
            P(None, None, "dp"),
            P(None, "dp", None),
            P(None, None, "dp"),
        ),
        check_vma=False,
    )
```

profile of v0, /device:TPU:0, one launch (start us, length us, event | category | flops | bytes accessed | tf_op | source)
XLA Modules:
  0.0 972.4 jit_solution(14850025663873997361)
XLA Ops:
  39.2 25.8 %all-gather.15.cloned.1.call-done = bf16[1536,768]{1,0:T(8,128)(2,1)} async-done(((bf16[192,768]{1,0:T(8,128)(2,1)}), bf16[1536,768]{1,0:T(8,128)(2,1)}) %all-gather.15.cloned.1.call-update) | async-done | bytes 2359312 | tf_op jit(solution)/shard_map/all_gather | solution.py:219
  74.2 78.8 %all-gather.13.cloned.1.call-done = bf16[768,3352]{1,0:T(8,128)(2,1)} async-done(((bf16[96,3352]{1,0:T(8,128)(2,1)}), bf16[768,3352]{1,0:T(8,128)(2,1)}) %all-gather.13.cloned.1.call-update) | async-done | bytes 5148688 | tf_op jit(solution)/shard_map/all_gather | solution.py:218
  153.0 5.9 fusion.279
  159.0 4.0 fusion.301
  178.7 6.5 fusion.300
  188.2 4.1 collective-permute-start
  194.7 8.9 fusion.77
  206.6 5.2 reshape.467
  212.1 6.0 fusion.121
  219.4 4.7 while.205
  231.8 5.3 reshape.460
  237.6 4.8 fusion.119
  246.7 9.8 %all-reduce.24 = (bf16[96]{0:T(256)(128)(2,1)S(1)}, bf16[96]{0:T(256)(128)(2,1)S(1)}) all-reduce(bf16[96]{0:T(256)(128)(2,1)S(1)} %dynamic-update-slice.1, bf16[96]{0:T(256)(128)(2,1)S(1)} %dynamic-update-slice), channel_id=4, replica_groups=mesh['dp'=8,'ctx'=4] {'ctx'}, use_global_device_ids=true, to_apply=%add.21 | all-reduce | flops 192 | bytes 768
  265.5 5.0 while.199
  270.5 4.3 fusion.306
  276.5 14.2 %bitcast_add_fusion.6 = f32[2,256,24,64]{1,3,2,0:T(8,128)S(1)} fusion(f32[2,256,24,64]{1,3,2,0:T(8,128)S(1)} %fusion.306, f32[2,256,256]{2,1,0:T(8,128)S(1)} %copy-done.105, f32[2,24,256]{2,1,0:T(8,128)S(1)} %copy-done.156, pred[256,256]{1,0:T(8,128)(4,1)S(1)} %copy-done.141, f32[2,256,24,64]{1,0,3,2:T(2,128)S(1)} %copy-done.4, ...), kind=kOutput, calls=%fused_computation.185 | convolution fusion | flops 2427715584 | bytes 10174464 | tf_op jit(solution)/shard_map/jvp(chqs,cshp->cqhp)/dot_general | solution.py:152
  299.2 4.2 fusion.303
  305.0 14.0 %bitcast_add_fusion.7 = f32[2,256,24,64]{1,3,2,0:T(8,128)S(1)} fusion(f32[2,256,24,64]{1,3,2,0:T(8,128)S(1)} %fusion.303, f32[2,256,256]{2,1,0:T(8,128)S(1)} %copy-done.102, f32[2,24,256]{2,1,0:T(8,128)S(1)} %copy-done.153, pred[256,256]{1,0:T(8,128)(4,1)S(1)} %copy-done.142, f32[2,256,24,64]{1,0,3,2:T(2,128)S(1)} %copy-done.12, ...), kind=kOutput, calls=%fused_computation.191 | convolution fusion | flops 2427715584 | bytes 10174464 | tf_op jit(solution)/shard_map/jvp(chqs,cshp->cqhp)/dot_general | solution.py:152
  324.8 8.6 multiply_reduce_fusion.9
  333.4 13.9 %fusion.97 = (bf16[512,1536]{0,1:T(8,128)(2,1)}, f32[512,1536]{0,1:T(8,128)}, bf16[512,1536]{0,1:T(8,128)(2,1)}, bf16[512,1536]{0,1:T(8,128)(2,1)}, f32[512,1536]{0,1:T(8,128)}, /*index=5*/bf16[512,1536]{0,1:T(8,128)(2,1)}) fusion(f32[512,3072]{0,1:T(8,128)S(1)} %bitcast.673, f32[512,1536]{0,1:T(8,128)} %get-tuple-element.1469, ...), kind=kLoop, calls=%fused_computation.169 | loop fusion | flops 34603008 | bytes 44060672 | tf_op jit(solution)/shard_map/convert.10
  347.4 5.5 reshape.488
  352.9 7.8 fusion.181
  360.7 14.8 %fusion.101 = f32[2,24,256,256]{3,2,1,0:T(8,128)} fusion(f32[2,256,24,64]{1,0,3,2:T(2,128)S(1)} %copy-done.5, f32[2,256,24,64]{1,0,3,2:T(2,128)} %reshape.488, f32[2,256,24]{1,2,0:T(8,128)S(1)} %bitcast.728), kind=kOutput, calls=%fused_computation.177 | convolution fusion | flops 2416705536 | bytes 18923520 | tf_op jit(solution)/shard_map/transpose(jvp(chqs,cshp->cqhp))/dot_general | solution.py:152
  375.6 4.0 fusion.110
  382.6 5.2 reshape.474
  387.9 8.3 fusion.178
  396.3 25.2 %fusion.39 = (f32[2,24,256]{2,1,0:T(8,128)}, f32[2,24,256]{2,1,0:T(8,128)}, f32[2,256,256]{2,1,0:T(8,128)S(1)}, f32[2,256,256]{2,1,0:T(8,128)S(1)}, f32[2,24,256]{2,1,0:T(8,128)}, /*index=5*/f32[2,24,256]{2,1,0:T(8,128)}) fusion(f32[2,256,256]{2,1,0:T(8,128)S(1)} %copy-done.103, f32[2,24,256]{2,1,0:T(8,128)S(1)} %copy-done.154, ...), kind=kOutput, calls=%fused_computation.87 | convolution fusion | flops 2473017344 | bytes 21381120 | tf_op jit(solution)/shard_map/transpose(jvp(chqs,cshp->cqhp))/dot_general | solution.py:152
  426.4 7.1 while.207
  444.3 4.0 copy.383
  448.4 5.1 reshape.564
  453.5 6.0 fusion.114
  461.0 5.1 while.206
  466.9 11.8 %fusion.29 = f32[2,24,64,256]{3,2,1,0:T(8,128)S(1)} fusion(f32[2,256,256]{2,1,0:T(8,128)S(1)} %copy-done.107, f32[2,24,256]{2,1,0:T(8,128)S(1)} %copy-done.158, pred[256,256]{1,0:T(8,128)(4,1)S(1)} %copy-done.144, f32[2,256,24,64]{1,0,3,2:T(2,128)} %reshape.488), kind=kOutput, calls=%fused_computation.80 | convolution fusion | flops 2425356288 | bytes 6930432 | tf_op jit(solution)/shard_map/transpose(jvp(chqs,cshp->cqhp))/dot_general | solution.py:152
  483.4 12.1 %fusion.34 = f32[2,24,64,256]{3,2,1,0:T(8,128)S(1)} fusion(f32[2,256,256]{2,1,0:T(8,128)S(1)} %copy-done.104, f32[2,24,256]{2,1,0:T(8,128)S(1)} %copy-done.155, pred[256,256]{1,0:T(8,128)(4,1)S(1)} %copy-done.144, f32[2,256,24,64]{1,0,3,2:T(2,128)} %reshape.474), kind=kOutput, calls=%fused_computation.84 | convolution fusion | flops 2425356288 | bytes 6930432 | tf_op jit(solution)/shard_map/transpose(jvp(chqs,cshp->cqhp))/dot_general | solution.py:152
  503.0 5.0 reduce-window.54
  512.5 5.0 reduce-window.46
  518.3 4.1 copy.405
  525.1 4.5 multiply_reduce_fusion.5
  538.9 37.1 %reduce-scatter.15.cloned.1.call-done = f32[192,128]{1,0:T(8,128)} async-done(((f32[1536,128]{1,0:T(8,128)}), f32[192,128]{1,0:T(8,128)}) %reduce-scatter.15.cloned.1.call-update) | async-done | bytes 98320
  578.1 18.2 %all-gather.23.cloned.1.call-done = bf16[96,64,128]{2,1,0:T(8,128)(2,1)} async-done(((bf16[24,64,128]{2,1,0:T(8,128)(2,1)}), bf16[96,64,128]{2,1,0:T(8,128)(2,1)}) %all-gather.23.cloned.1.call-update) | async-done | bytes 1572880 | tf_op jit(solution)/shard_map/all_gather | solution.py:50
  596.4 4.0 while.202
  604.9 8.4 fusion.176
  613.3 4.5 broadcast_multiply_fusion.10
  617.9 4.0 while.200
  624.1 4.9 while.201
  629.5 8.1 fusion.177
  637.7 4.9 broadcast_multiply_fusion.11
  645.0 4.4 copy.304
  658.0 9.5 fusion.104
  667.5 11.0 %broadcast_multiply_fusion.3 = (f32[512,1792]{0,1:T(8,128)S(1)}, f32[512,1792]{0,1:T(8,128)}, f32[512,1792]{0,1:T(8,128)S(1)}, f32[512,1792]{0,1:T(8,128)}) fusion(f32[1792]{0:T(1024)S(1)} %copy-done.138, f32[512,1792]{0,1:T(8,128)} %get-tuple-element.1406, f32[512,1536]{0,1:T(8,128)} %get-tuple-element.1465, f32[512,128]{0,1:T(8,128)S(1)} %copy.372, ...), kind=kLoop, calls=%fused_computation.252 | loop fusion | flops 22020096 | bytes 29367296 | tf_op jit(solution)/shard_map/transpose(jvp())/mul | solution.py:100
  678.6 6.1 broadcast_multiply_fusion.4
  689.4 10.0 %pad_add_fusion.1 = f32[515,1792]{0,1:T(8,128)} fusion(f32[512,1792]{0,1:T(8,128)} %copy-done.17, f32[512,1792]{0,1:T(8,128)} %copy-done.18, f32[512,1792]{0,1:T(8,128)} %copy-done.19, f32[512,1792]{0,1:T(8,128)S(1)} %get-tuple-element.1397), kind=kLoop, calls=%fused_computation.119 | loop fusion | flops 2768640 | bytes 18371584 | tf_op jit(solution)/shard_map/transpose(jvp())/add_any | solution.py:98
  702.5 7.8 pad_add_fusion
  715.4 6.7 multiply_reduce_fusion.2
  722.4 5.2 reduce-window.56
  728.0 6.7 multiply_reduce_fusion.3
  735.6 5.0 reduce-window.50
  765.1 6.5 add_multiply_fusion
  771.6 7.5 fusion.151
  779.2 43.3 %reduce-scatter.13.cloned.1.call-done = f32[96,128]{1,0:T(8,128)} async-done(((f32[768,128]{1,0:T(8,128)}), f32[96,128]{1,0:T(8,128)}) %reduce-scatter.13.cloned.1.call-update) | async-done | bytes 49168
  824.4 4.0 fusion.143
  828.4 61.7 %reduce-scatter.11.cloned.1.call-done = f32[8,16,384]{2,1,0:T(8,128)} async-done(((f32[8,16,3072]{2,1,0:T(8,128)}), f32[8,16,384]{2,1,0:T(8,128)}) %reduce-scatter.11.cloned.1.call-update) | async-done | bytes 196624 | tf_op jit(solution)/shard_map/reduce_scatter | solution.py:294
  893.9 29.6 %all-reduce.28.cloned.1.call-done = (f32[8,96,16]{1,2,0:T(8,128)}, f32[8,16,96]{2,1,0:T(8,128)}) async-done(((f32[8,96,16]{1,2,0:T(8,128)}, f32[8,16,96]{2,1,0:T(8,128)}), (f32[8,96,16]{1,2,0:T(8,128)}, f32[8,16,96]{2,1,0:T(8,128)})) %all-reduce.28.cloned.1.call-update) | async-done | bytes 98320 | tf_op jit(solution)/shard_map/psum | solution.py:291
  923.5 35.5 %all-reduce.30.cloned.1.call-done = (f32[8,16,384]{2,1,0:T(8,128)}, f32[8,192,16]{1,2,0:T(8,128)}) async-done(((f32[8,16,384]{2,1,0:T(8,128)}, f32[8,192,16]{1,2,0:T(8,128)}), (f32[8,16,384]{2,1,0:T(8,128)}, f32[8,192,16]{1,2,0:T(8,128)})) %all-reduce.30.cloned.1.call-update) | async-done | bytes 294928 | tf_op jit(solution)/shard_map/psum | solution.py:291
  (854 shorter events, 265.7 us)
Async XLA Ops:
  7.2 27.9 %copy-start = (bf16[8,16,3072]{2,1,0:T(8,128)(2,1)S(1)}, bf16[8,16,3072]{2,1,0:T(8,128)(2,1)}, u32[]{:S(2)}) copy-start(bf16[8,16,3072]{2,1,0:T(8,128)(2,1)} %param.56) | copy-start | bytes 2359300
  7.2 12.3 %copy-start.237 = (u32[32]{0:T(128)S(1)}, u32[32]{0:T(128)}, u32[]{:S(2)}) copy-start(u32[32]{0:T(128)} %constant.420) | copy-start | bytes 388
  7.2 15.4 %copy-start.210 = (s32[2]{0:T(128)S(1)}, s32[2]{0:T(128)}, u32[]{:S(2)}) copy-start(s32[2]{0:T(128)} %param.44) | copy-start | bytes 28
  7.2 19.8 %copy-start.169 = (f32[4,1792]{1,0:T(4,128)S(1)}, f32[4,1792]{1,0:T(4,128)}, u32[]{:S(2)}) copy-start(f32[4,1792]{1,0:T(4,128)} %param.48) | copy-start | bytes 86020
  7.2 22.3 %copy-start.227 = (f32[24]{0:T(128)S(1)}, f32[24]{0:T(128)}, u32[]{:S(2)}) copy-start(f32[24]{0:T(128)} %param.51) | copy-start | bytes 292
  7.2 22.9 %copy-start.101 = (bf16[8,16,768]{2,1,0:T(8,128)(2,1)S(1)}, bf16[8,16,768]{2,1,0:T(8,128)(2,1)}, u32[]{:S(2)}) copy-start(bf16[8,16,768]{2,1,0:T(8,128)(2,1)} %param.58) | copy-start | bytes 589828
  7.2 57.8 %all-gather.15.cloned.1.call-start = ((), (), s32[]{:S(2)}) async-start(), calls=%async_computation.5 | async-start | bytes 2654208 | tf_op jit(solution)/shard_map/all_gather | solution.py:219
  8.0 145.0 %all-gather.13.cloned.1.call-start = ((), (), s32[]{:S(2)}) async-start(), calls=%async_computation.4 | async-start | bytes 5971968 | tf_op jit(solution)/shard_map/all_gather | solution.py:218
  8.7 255.2 %all-gather.19.cloned.1.call-start = ((), (), s32[]{:S(2)}) async-start(), calls=%async_computation.7 | async-start | bytes 1966080 | tf_op jit(solution)/shard_map/all_gather | solution.py:28
  12.1 25.6 %copy-start.97 = (bf16[1,768,16]{2,1,0:T(8,128)(2,1)}, bf16[1,768,16]{2,1,0:T(8,128)(2,1)S(1)}, u32[]{:S(2)}) copy-start(bf16[1,768,16]{2,1,0:T(8,128)(2,1)S(1)} %copy.330) | copy-start | bytes 73732
  14.1 24.1 %copy-start.99 = (bf16[1,768,16]{2,1,0:T(8,128)(2,1)}, bf16[1,768,16]{2,1,0:T(8,128)(2,1)S(1)}, u32[]{:S(2)}) copy-start(bf16[1,768,16]{2,1,0:T(8,128)(2,1)S(1)} %copy.320) | copy-start | bytes 73732
  16.4 55.6 %copy-start.53 = (bf16[1,1536,16]{2,1,0:T(8,128)(2,1)}, bf16[1,1536,16]{2,1,0:T(8,128)(2,1)S(1)}, u32[]{:S(2)}) copy-start(bf16[1,1536,16]{2,1,0:T(8,128)(2,1)S(1)} %copy.335) | copy-start | bytes 147460
  19.5 313.9 %copy-start.129 = (f32[1536]{0:T(1024)}, f32[1536]{0:T(1024)S(1)}, u32[]{:S(2)}) copy-start(f32[1536]{0:T(1024)S(1)} %mul.1125) | copy-start | bytes 18436
  19.5 14.6 %copy-start.85 = (bf16[2,512,768]{2,1,0:T(8,128)(2,1)S(1)}, bf16[2,512,768]{2,1,0:T(8,128)(2,1)}, u32[]{:S(2)}) copy-start(bf16[2,512,768]{2,1,0:T(8,128)(2,1)} %param.43) | copy-start | bytes 4718596
  27.7 167.0 %copy-start.131 = (f32[1792]{0:T(1024)}, f32[1792]{0:T(1024)S(1)}, u32[]{:S(2)}) copy-start(f32[1792]{0:T(1024)S(1)} %get-tuple-element.1221) | copy-start | bytes 21508
  36.4 122.6 %copy-start.112 = (bf16[1,16,3072]{2,0,1:T(2,128)(2,1)}, bf16[1,16,3072]{2,0,1:T(2,128)(2,1)S(1)}, u32[]{:S(2)}) copy-start(bf16[1,16,3072]{2,0,1:T(2,128)(2,1)S(1)} %fusion.188) | copy-start | bytes 294916
  37.7 141.0 %copy-start.114 = (bf16[1,16,3072]{2,0,1:T(2,128)(2,1)}, bf16[1,16,3072]{2,0,1:T(2,128)(2,1)S(1)}, u32[]{:S(2)}) copy-start(bf16[1,16,3072]{2,0,1:T(2,128)(2,1)S(1)} %fusion.190) | copy-start | bytes 294916
  37.7 27.3 %copy-start.212 = (bf16[512]{0:T(512)(128)(2,1)S(1)}, bf16[512]{0:T(512)(128)(2,1)}, u32[]{:S(2)}) copy-start(bf16[512]{0:T(512)(128)(2,1)} %copy-done.211) | copy-start | bytes 3076
  38.2 120.8 %copy-start.184 = (bf16[512,16]{0,1:T(8,128)(2,1)}, bf16[512,16]{0,1:T(8,128)(2,1)S(1)}, u32[]{:S(2)}) copy-start(bf16[512,16]{0,1:T(8,128)(2,1)S(1)} %convolution_convert_fusion.3) | copy-start | bytes 49156
  39.2 29.4 %copy-start.215 = (bf16[512]{0:T(512)(128)(2,1)S(1)}, bf16[512]{0:T(512)(128)(2,1)}, u32[]{:S(2)}) copy-start(bf16[512]{0:T(512)(128)(2,1)} %copy-done.214) | copy-start | bytes 3076
  72.0 81.0 %copy-start.196 = (f32[512]{0:T(512)S(1)}, f32[512]{0:T(512)}, u32[]{:S(2)}) copy-start(f32[512]{0:T(512)} %copy-done.195) | copy-start | bytes 6148
  72.0 81.0 %copy-start.225 = (f32[768]{0:T(1024)S(1)}, f32[768]{0:T(1024)}, u32[]{:S(2)}) copy-start(f32[768]{0:T(1024)} %param.46) | copy-start | bytes 9220
  158.9 12.5 %copy-start.51 = (f32[512,3352]{0,1:T(8,128)}, f32[512,3352]{0,1:T(8,128)S(1)}, u32[]{:S(2)}) copy-start(f32[512,3352]{0,1:T(8,128)S(1)} %fusion.279) | copy-start | bytes 20594692
  166.8 25.4 %collective-permute-start.1 = (bf16[3,1792]{0,1:T(8,128)(2,1)S(1)}, bf16[3,1792]{0,1:T(8,128)(2,1)S(1)}, u32[]{:S(2)}, u32[]{:S(2)}) collective-permute-start(bf16[3,1792]{0,1:T(8,128)(2,1)S(1)} %pad_maximum_fusion.14), channel_id=1, source_target_pairs={{0,1},{1,2},{2,3},{4,5},{5,6},{6,7},{8,9},{9,10},{10,11},{12,13},{... | collective-permute-start | bytes 32264 | tf_op jit(solution)/shard_map/ppermute | solution.py:22
  174.2 12.7 %copy-start.80 = (f32[512,24]{0,1:T(8,128)}, f32[512,24]{0,1:T(8,128)S(1)}, u32[]{:S(2)}) copy-start(f32[512,24]{0,1:T(8,128)S(1)} %get-tuple-element.1477) | copy-start | bytes 147460
  174.2 13.3 %copy-start.78 = (f32[512,24]{0,1:T(8,128)}, f32[512,24]{0,1:T(8,128)S(1)}, u32[]{:S(2)}) copy-start(f32[512,24]{0,1:T(8,128)S(1)} %get-tuple-element.1408) | copy-start | bytes 147460
  186.2 51.4 %copy-start.93 = (f32[2,256,24]{1,2,0:T(8,128)}, f32[2,256,24]{1,2,0:T(8,128)S(1)}, u32[]{:S(2)}) copy-start(f32[2,256,24]{1,2,0:T(8,128)S(1)} %get-tuple-element.1448) | copy-start | bytes 147460
  186.9 25.2 %copy-start.95 = (f32[2,256,24]{1,2,0:T(8,128)}, f32[2,256,24]{1,2,0:T(8,128)S(1)}, u32[]{:S(2)}) copy-start(f32[2,256,24]{1,2,0:T(8,128)S(1)} %get-tuple-element.1452) | copy-start | bytes 147460
  188.2 5.5 collective-permute-start
  224.9 70.2 %all-gather.17.cloned.1.call-start = ((), (), s32[]{:S(2)}) async-start(), calls=%async_computation.6 | async-start | bytes 1966080 | tf_op jit(solution)/shard_map/all_gather | solution.py:28
  237.4 25.1 %copy-start.64 = (f32[2,256,128]{2,1,0:T(8,128)}, f32[2,256,128]{2,1,0:T(8,128)S(1)}, u32[]{:S(2)}) copy-start(f32[2,256,128]{2,1,0:T(8,128)S(1)} %copy.246) | copy-start | bytes 786436
  246.2 17.7 %copy-start.204 = (f32[2,24]{1,0:T(2,128)}, f32[2,24]{1,0:T(2,128)S(1)}, u32[]{:S(2)}) copy-start(f32[2,24]{1,0:T(2,128)S(1)} %get-tuple-element.2242) | copy-start | bytes 580
  262.5 274.7 %reduce-scatter.17.cloned.1.call-start = ((), (), s32[]{:S(2)}) async-start(), calls=%async_computation.13 | async-start | bytes 442368
  270.4 20.3 %copy-start.165 = (f32[2,24]{1,0:T(2,128)}, f32[2,24]{1,0:T(2,128)S(1)}, u32[]{:S(2)}) copy-start(f32[2,24]{1,0:T(2,128)S(1)} %get-tuple-element.2428) | copy-start | bytes 580
  299.1 20.0 %copy-start.163 = (f32[2,24]{1,0:T(2,128)}, f32[2,24]{1,0:T(2,128)S(1)}, u32[]{:S(2)}) copy-start(f32[2,24]{1,0:T(2,128)S(1)} %get-tuple-element.2426) | copy-start | bytes 580
  299.1 20.0 %copy-start.235 = (f32[2,24,1,1]{1,3,2,0:T(1,128)}, f32[2,24,1,1]{1,3,2,0:T(1,128)S(1)}, u32[]{:S(2)}) copy-start(f32[2,24,1,1]{1,3,2,0:T(1,128)S(1)} %get-tuple-element.2185) | copy-start | bytes 580
  299.1 24.4 %slice-start = ((s8[6291456]{0:T(1024)(128)(4,1)}), s8[4194304]{0:T(1024)(128)(4,1)S(1)}, s32[]{:S(2)}) async-start(s8[6291456]{0:T(1024)(128)(4,1)} %bitcast.672), calls=%async_computation.16 | async-start | bytes 8388608
  299.2 24.4 %slice-start.2 = ((s8[6291456]{0:T(1024)(128)(4,1)}), s8[4194304]{0:T(1024)(128)(4,1)S(1)}, s32[]{:S(2)}) async-start(s8[6291456]{0:T(1024)(128)(4,1)} %bitcast.674), calls=%async_computation.18 | async-start | bytes 8388608
  305.0 18.6 %slice-start.1 = ((s8[6291456]{0:T(1024)(128)(4,1)}), s8[2097152]{0:T(1024)(128)(4,1)S(1)}, s32[]{:S(2)}) async-start(s8[6291456]{0:T(1024)(128)(4,1)} %bitcast.672), calls=%async_computation.17 | async-start | bytes 4194304
  305.0 18.6 %slice-start.3 = ((s8[6291456]{0:T(1024)(128)(4,1)}), s8[2097152]{0:T(1024)(128)(4,1)S(1)}, s32[]{:S(2)}) async-start(s8[6291456]{0:T(1024)(128)(4,1)} %bitcast.674), calls=%async_computation.19 | async-start | bytes 4194304
  360.7 14.8 %copy-start.6 = (f32[2,256,24,64]{1,0,3,2:T(2,128)S(1)}, f32[2,256,24,64]{1,0,3,2:T(2,128)}, u32[]{:S(2)}) copy-start(f32[2,256,24,64]{1,0,3,2:T(2,128)} %reshape.488) | copy-start | bytes 9437188
  360.7 14.8 %copy-start.59 = (f32[2,256,128,1]{2,1,3,0:T(8,128)S(1)}, f32[2,256,128,1]{2,1,3,0:T(8,128)}, u32[]{:S(2)}) copy-start(f32[2,256,128,1]{2,1,3,0:T(8,128)} %copy.334) | copy-start | bytes 786436
  396.2 25.2 %copy-start.66 = (f32[2,256,128]{2,1,0:T(8,128)S(1)}, f32[2,256,128]{2,1,0:T(8,128)}, u32[]{:S(2)}) copy-start(f32[2,256,128]{2,1,0:T(8,128)} %copy.259) | copy-start | bytes 786436
  396.2 25.2 %copy-start.92 = (f32[2,256,128]{2,1,0:T(8,128)S(1)}, f32[2,256,128]{2,1,0:T(8,128)}, u32[]{:S(2)}) copy-start(f32[2,256,128]{2,1,0:T(8,128)} %fusion.181) | copy-start | bytes 786436
  421.4 12.9 %copy-start.67 = (f32[2,256,256]{2,1,0:T(8,128)}, f32[2,256,256]{2,1,0:T(8,128)S(1)}, u32[]{:S(2)}) copy-start(f32[2,256,256]{2,1,0:T(8,128)S(1)} %get-tuple-element.1208) | copy-start | bytes 1572868
  444.1 131.9 %reduce-scatter.15.cloned.1.call-start = ((), (), s32[]{:S(2)}) async-start(), calls=%async_computation.12 | async-start | bytes 884736
  459.5 136.8 %all-gather.23.cloned.1.call-start = ((), (), s32[]{:S(2)}) async-start(), calls=%async_computation.9 | async-start | bytes 1966080 | tf_op jit(solution)/shard_map/all_gather | solution.py:50
  466.1 12.6 %copy-start.221 = (f32[2,24]{1,0:T(2,128)}, f32[2,24]{1,0:T(2,128)S(1)}, u32[]{:S(2)}) copy-start(f32[2,24]{1,0:T(2,128)S(1)} %get-tuple-element.1088) | copy-start | bytes 580
  483.4 134.4 %all-gather.21.cloned.1.call-start = ((), (), s32[]{:S(2)}) async-start(), calls=%async_computation.8 | async-start | bytes 1966080 | tf_op jit(solution)/shard_map/all_gather | solution.py:50
  524.5 298.0 %reduce-scatter.13.cloned.1.call-start = ((), (), s32[]{:S(2)}) async-start(), calls=%async_computation.11 | async-start | bytes 442368
  535.8 60.5 %copy-start.231 = (bf16[4,24]{1,0:T(4,128)(2,1)S(1)}, bf16[4,24]{1,0:T(4,128)(2,1)}, u32[]{:S(2)}) copy-start(bf16[4,24]{1,0:T(4,128)(2,1)} %copy-done.230) | copy-start | bytes 580
  702.5 12.2 %copy-start.173 = (f32[2,24]{1,0:T(2,128)S(1)}, f32[2,24]{1,0:T(2,128)}, u32[]{:S(2)}) copy-start(f32[2,24]{1,0:T(2,128)} %copy-done.172) | copy-start | bytes 580
  702.5 12.2 %copy-start.218 = (f32[2,24]{1,0:T(2,128)S(1)}, f32[2,24]{1,0:T(2,128)}, u32[]{:S(2)}) copy-start(f32[2,24]{1,0:T(2,128)} %copy-done.217) | copy-start | bytes 580
  710.6 30.1 %collective-permute-start.2 = (f32[3,1792]{1,0:T(4,128)S(1)}, f32[3,1792]{1,0:T(4,128)S(1)}, u32[]{:S(2)}, u32[]{:S(2)}) collective-permute-start(f32[3,1792]{1,0:T(4,128)S(1)} %copy.278), channel_id=1, source_target_pairs={{1,0},{2,1},{3,2},{5,4},{6,5},{7,6},{9,8},{10,9},{11,10},{13,12},{... | collective-permute-start | bytes 64520 | tf_op jit(solution)/shard_map/ppermute | solution.py:22
  713.3 34.4 %collective-permute-start.3 = (f32[3,1792]{1,0:T(4,128)S(1)}, f32[3,1792]{1,0:T(4,128)S(1)}, u32[]{:S(2)}, u32[]{:S(2)}) collective-permute-start(f32[3,1792]{1,0:T(4,128)S(1)} %copy.305), channel_id=1, source_target_pairs={{1,0},{2,1},{3,2},{5,4},{6,5},{7,6},{9,8},{10,9},{11,10},{13,12},{... | collective-permute-start | bytes 64520 | tf_op jit(solution)/shard_map/ppermute | solution.py:22
  715.4 12.5 %copy-start.171 = (f32[2,24]{1,0:T(2,128)S(1)}, f32[2,24]{1,0:T(2,128)}, u32[]{:S(2)}) copy-start(f32[2,24]{1,0:T(2,128)} %copy-done.170) | copy-start | bytes 580
  715.4 12.5 %copy-start.220 = (f32[2,24]{1,0:T(2,128)S(1)}, f32[2,24]{1,0:T(2,128)}, u32[]{:S(2)}) copy-start(f32[2,24]{1,0:T(2,128)} %copy-done.219) | copy-start | bytes 580
  715.4 12.5 %copy-start.222 = (f32[2,24]{1,0:T(2,128)S(1)}, f32[2,24]{1,0:T(2,128)}, u32[]{:S(2)}) copy-start(f32[2,24]{1,0:T(2,128)} %copy-done.221) | copy-start | bytes 580
  758.3 131.7 %reduce-scatter.11.cloned.1.call-start = ((), (), s32[]{:S(2)}) async-start(), calls=%async_computation.10 | async-start | bytes 1769472 | tf_op jit(solution)/shard_map/reduce_scatter | solution.py:294
  762.9 160.6 %all-reduce.28.cloned.1.call-start = ((), (), s32[]{:S(2)}) async-start(), calls=%async_computation.14 | async-start | bytes 262144 | tf_op jit(solution)/shard_map/psum | solution.py:291
  771.6 52.7 %copy-start.181 = (f32[512]{0:T(512)S(1)}, f32[512]{0:T(512)}, u32[]{:S(2)}) copy-start(f32[512]{0:T(512)} %get-tuple-element.1494) | copy-start | bytes 6148
  771.6 52.7 %copy-start.183 = (f32[512]{0:T(512)S(1)}, f32[512]{0:T(512)}, u32[]{:S(2)}) copy-start(f32[512]{0:T(512)} %get-tuple-element.1495) | copy-start | bytes 6148
  824.3 134.7 %all-reduce.30.cloned.1.call-start = ((), (), s32[]{:S(2)}) async-start(), calls=%async_computation.15 | async-start | bytes 655360 | tf_op jit(solution)/shard_map/psum | solution.py:291
  890.1 75.0 %copy-start.1 = (bf16[8,16,3072]{2,1,0:T(8,128)(2,1)S(1)}, bf16[8,16,3072]{2,1,0:T(8,128)(2,1)}, u32[]{:S(2)}) copy-start(bf16[8,16,3072]{2,1,0:T(8,128)(2,1)} %param.56) | copy-start | bytes 2359300
  (200 other events, 987.8 us)
Sparse Core Ops, SparseCore 0:
  10.3 54.7 all-gather.14
  67.2 85.7 all-gather.12
  225.1 22.7 all-gather.18
  262.6 18.6 all-gather.16
  444.2 67.0 reduce-scatter.16
  514.5 61.4 reduce-scatter.14
  577.6 18.6 all-gather.22
  597.9 19.6 all-gather.20
  758.3 64.1 reduce-scatter.12
  826.2 63.8 reduce-scatter.10
  893.0 30.4 all-reduce.27
  926.5 32.3 all-reduce.29
where the time goes:
time: 984 us; the launch traced here: 972 us
  waiting for transfers between devices  332 us (34%)
  matrix products  254 us (26%)
  other arithmetic  184 us (19%)
  local copies, waits for them, and re-layouts  162 us (16%)
  between operations  18.7 us (2%)
    dot_general x6, matrix products, block_outputs(): inside = jnp.einsum('chqs,cshp->cqhp', weights, x_blocks, precision=precise)  92.1 us
    unnamed x15, waiting for transfers between devices  81.9 us
    all_gather x1, waiting for transfers between devices, shards(): lax.all_gather(w_in, 'dp', axis=0, tiled=True)  78.8 us
    unnamed x509, local copies, waits for them, and re-layouts  68.6 us
    psum x2, waiting for transfers between devices, shards(): lax.psum((gradients[0], gradients[1], gradients[2], gradients[3]), 'ctx')  65.1 us
    reduce_scatter x1, waiting for transfers between devices, shards(): lax.psum_scatter(summed[1], 'dp', scatter_dimension=2, tiled=True)  61.7 us
    another operation x22, other arithmetic  46.2 us
    dot_general x12, matrix products, contract_cols(): lax.dot_general(left, right, (((1,), (1,)), ((), ())), preferred_element_...  36.7 us
  transfers between devices with their start and end apart: 16, of which 9 were waited for; matrix products, arithmetic and copies ran while one was open for 30% of the time, Pallas kernels for 0%

commit v1 on v0

v1 whole, which is shorter than its diff:
```python
import functools

import jax
import jax.numpy as jnp
from jax import lax
from jax.experimental import pallas as pl
from jax.experimental.pallas import tpu as pltpu
from jax.sharding import PartitionSpec as P

HEADS = 24
HDIM = 64
NSTATE = 128
INNER = 1536
CONV_CH = 1792
ZX = 3072
DM = 768
RANK = 16
CHUNK = 128
TILE = 256
RIM = 16
GROUP = 32
LANES = 128
VMEM_LIMIT = 60 * 1024 * 1024

epsilon = 1e-05
bf16 = jnp.bfloat16
f32 = jnp.float32


def dot(left, right):
    return jnp.dot(left, right, preferred_element_type=f32)


def dot_t(left, right):
    return lax.dot_general(
        left, right, (((1,), (1,)), ((), ())), preferred_element_type=f32
    )


def dot_precise(left, right):
    return jnp.dot(
        left, right, preferred_element_type=f32, precision=lax.Precision.HIGHEST
    )


def parts_of(v):
    lane = lax.broadcasted_iota(jnp.int32, v.shape, 1)
    high = v.astype(bf16).astype(f32)
    rest = v - high
    middle = rest.astype(bf16).astype(f32)
    kept = jnp.where(lane < GROUP, high, jnp.where(lane < 2 * GROUP, middle, rest - middle))
    return jnp.where(lane < 3 * GROUP, kept, 0.0).astype(bf16)


def causal(rows):
    t = lax.broadcasted_iota(jnp.int32, (rows, rows), 0)
    s = lax.broadcasted_iota(jnp.int32, (rows, rows), 1)
    return t >= s


def lane_tile(t, width=TILE):
    return pl.ds(t * width, width)


def norm_kernel(ids, x_ref, rim_ref, gain_ref, a_ref, nrm_ref, nrim_ref, lat_ref, lrim_ref):
    def normed(x):
        x = x.astype(f32)
        mean = jnp.mean(x * x, -1, keepdims=True)
        return (x * lax.rsqrt(mean + epsilon) * gain_ref[...]).astype(bf16)

    rows = x_ref.shape[1]
    strip = 64

    def body(i, carry):
        r = pl.ds(pl.multiple_of(i * strip, strip), strip)
        nrm_ref[0, r, :] = normed(x_ref[0, r, :])
        return carry

    lax.fori_loop(0, rows // strip, body, 0)
    nrim_ref[0] = normed(rim_ref[0])
    lat_ref[0] = dot(nrm_ref[0], a_ref[0]).astype(bf16)
    lrim_ref[0] = dot(nrim_ref[0], a_ref[0]).astype(bf16)


def norm_call(ids, tokens, rim, gain, in_a):
    seqs, rows, _ = tokens.shape
    block = lambda *shape: pl.BlockSpec((1,) + shape, lambda s, ids: (s, 0, 0))
    return pl.pallas_call(
        norm_kernel,
        grid_spec=pltpu.PrefetchScalarGridSpec(
            num_scalar_prefetch=1,
            grid=(seqs,),
            in_specs=[
                block(rows, DM),
                block(RIM, DM),
                pl.BlockSpec((1, DM), lambda s, ids: (0, 0)),
                pl.BlockSpec((1, DM, RANK), lambda s, ids: (ids[s], 0, 0)),
            ],
            out_specs=[block(rows, DM), block(RIM, DM), block(rows, RANK), block(RIM, RANK)],
        ),
        out_shape=[
            jax.ShapeDtypeStruct((seqs, rows, DM), bf16),
            jax.ShapeDtypeStruct((seqs, RIM, DM), bf16),
            jax.ShapeDtypeStruct((seqs, rows, RANK), bf16),
            jax.ShapeDtypeStruct((seqs, RIM, RANK), bf16),
        ],
        compiler_params=pltpu.CompilerParams(vmem_limit_bytes=VMEM_LIMIT),
        name="norm",
    )(ids, tokens, rim, gain, in_a)


def front_kernel(
    ids, nrm_ref, nrim_ref, lat_ref, lrim_ref, wx_ref, wdt_ref, bx_ref, cw_ref, cb_ref, dtb_ref,
    rate_ref, expand_ref, act_ref, dact_ref, dt_ref, cum_ref, sig_ref, pay_ref,
    nrm_s, lat_s, xs, bt_s, w_s,
):
    rows = nrm_ref.shape[1]
    nrm_s[0:RIM, :] = nrim_ref[0]
    nrm_s[RIM:, :] = nrm_ref[0]
    lat_s[0:RIM, :] = lrim_ref[0]
    lat_s[RIM:, :] = lat_ref[0]
    raw = dot(nrm_ref[0], wdt_ref[...]) + dtb_ref[...]
    step = jnp.maximum(raw, 0.0) + jnp.log1p(jnp.exp(-jnp.abs(raw)))
    dt_ref[...] = step
    sig_ref[...] = 1.0 / (1.0 + jnp.exp(-raw))
    logs = step * rate_ref[...]
    lower = causal(CHUNK).astype(f32)
    before = jnp.zeros((1, LANES), f32)
    whole = []
    for c in range(rows // CHUNK):
        r = slice(c * CHUNK, (c + 1) * CHUNK)
        cum = dot_precise(lower, logs[r])
        cum_ref[r, :] = cum
        whole.append(cum + before)
        before = before + cum[CHUNK - 1 : CHUNK]
    for c in range(rows // CHUNK):
        r = slice(c * CHUNK, (c + 1) * CHUNK)
        w_s[r, :] = parts_of(jnp.exp(before - whole[c]) * step[r])
    total = parts_of(jnp.broadcast_to(jnp.exp(before), (8, LANES)))

    def tile_in(cols, base, out_cols, state):
        xs[...] = base.astype(bf16).astype(f32)
        weights = [cw_ref[j : j + 1, cols] for j in range(4)]
        bias = cb_ref[:, cols]
        strip = 64
        for i in range(rows // strip):
            at = RIM + i * strip
            pre = bias + weights[0] * xs[at - 3 : at - 3 + strip, :]
            for j in range(1, 4):
                pre = pre + weights[j] * xs[at - 3 + j : at - 3 + j + strip, :]
            gate = 1.0 / (1.0 + jnp.exp(-pre))
            act = pre * gate
            r = slice(i * strip, (i + 1) * strip)
            act_ref[r, out_cols] = act.astype(bf16)
            dact_ref[r, out_cols] = (gate + act * (1.0 - gate)).astype(bf16)

    last = slice(INNER, CONV_CH)
    tile_in(last, dot(nrm_s[...], wx_ref[:, last]), last, None)
    bt_s[...] = jnp.transpose(act_ref[:, INNER : INNER + NSTATE].astype(f32)).astype(bf16)

    def tile_body(t, carry):
        cols = pl.ds(pl.multiple_of(t * TILE, TILE), TILE)
        base = dot(nrm_s[...], wx_ref[:, cols]) + dot(lat_s[...], bx_ref[0, :, cols])
        tile_in(cols, base, cols, None)
        scaled = (act_ref[:, cols].astype(f32) * dot(w_s[...], expand_ref[:, cols])).astype(bf16)
        pay_ref[0:NSTATE, cols] = dot(bt_s[...], scaled).astype(bf16)
        decay = dot(total, expand_ref[:, cols])
        high = decay.astype(bf16)
        row = lax.broadcasted_iota(jnp.int32, (RIM, TILE), 0)
        low = decay - high.astype(f32)
        both = jnp.where(row == 0, high.astype(f32)[0:1], jnp.where(row == 1, low[0:1], 0.0))
        pay_ref[NSTATE:, cols] = both.astype(bf16)
        return carry

    lax.fori_loop(0, INNER // TILE, tile_body, 0)


def front_call(seq, ids, nrm, nrim, lat, lrim, wx, wdt, in_b, conv_w, conv_b, dtb, rate, expand):
    rows = nrm.shape[1]
    block = lambda *shape: pl.BlockSpec((1,) + shape, lambda i, ids: (seq, 0, 0))
    whole = lambda a: pl.BlockSpec(a.shape, lambda i, ids: (0,) * a.ndim)
    outs = [
        ((rows, CONV_CH), bf16),
        ((rows, CONV_CH), bf16),
        ((rows, LANES), f32),
        ((rows, LANES), f32),
        ((rows, LANES), f32),
        ((NSTATE + RIM, INNER), bf16),
    ]
    return pl.pallas_call(
        front_kernel,
        grid_spec=pltpu.PrefetchScalarGridSpec(
            num_scalar_prefetch=1,
            grid=(1,),
            in_specs=[
                block(rows, DM),
                block(RIM, DM),
                block(rows, RANK),
                block(RIM, RANK),
                whole(wx),
                whole(wdt),
                pl.BlockSpec((1, RANK, INNER), lambda i, ids: (ids[seq], 0, 1)),
                whole(conv_w),
                whole(conv_b),
                whole(dtb),
                whole(rate),
                whole(expand),
            ],
            out_specs=[pl.BlockSpec(s, lambda i, ids: (0, 0)) for s, _ in outs],
            scratch_shapes=[
                pltpu.VMEM((rows + RIM, DM), bf16),
                pltpu.VMEM((rows + RIM, RANK), bf16),
                pltpu.VMEM((rows + RIM, TILE), f32),
                pltpu.VMEM((NSTATE, rows), bf16),
                pltpu.VMEM((rows, LANES), bf16),
            ],
        ),
        out_shape=[jax.ShapeDtypeStruct(s, d) for s, d in outs],
        compiler_params=pltpu.CompilerParams(vmem_limit_bytes=VMEM_LIMIT),
        name="front",
    )(ids, nrm, nrim, lat, lrim, wx, wdt, in_b, conv_w, conv_b, dtb, rate, expand)


def decayed(cum, cum_t, heads, masked):
    out = []
    for h in heads:
        gap = jnp.minimum(cum[:, h : h + 1] - cum_t[h : h + 1, :], 0.0)
        out.append(jnp.exp(gap))
    return out


def split_heads(pair):
    lane = lax.broadcasted_iota(jnp.int32, pair.shape, 1)
    zero = jnp.zeros_like(pair)
    first = jnp.where(lane < HDIM, pair, zero)
    second = jnp.where(lane < HDIM, zero, pair)
    return jnp.concatenate([first, second], axis=0)


def middle_kernel(
    ids, lens, x_ref, cot_ref, nrm_ref, lat_ref, act_ref, dt_ref, cum_ref, h_ref, wg_ref, bg_ref, wo_ref,
    oa_ref, ob_ref, skip_ref, gain_ref, expand_ref,
    out_ref, dy_ref, dg_ref, hc_ref, rowt_ref, pay_ref, tb_ref, ta_ref,
    gate_s, y_s, z_s, dh_s, hid_s, r_s, state_s, grad_s, run_s, prod_s, *, seq,
):
    step = pl.program_id(0)
    rows = act_ref.shape[0]
    strip = 16

    @pl.when(step == 0)
    def _():
        state_s[...] = h_ref[...]
        grad_s[...] = jnp.zeros_like(grad_s)
        run_s[...] = jnp.ones_like(run_s)
        tb_ref[...] = jnp.zeros_like(tb_ref)
        ta_ref[...] = jnp.zeros_like(ta_ref)

    gate_s[...] = dot(nrm_ref[0], wg_ref[...]) + dot(lat_ref[0], bg_ref[0])
    position = step * rows + lax.broadcasted_iota(jnp.int32, (rows, 1), 0)
    valid = position < lens[seq]
    g = jnp.where(valid, cot_ref[0], jnp.zeros((), bf16))
    d_lat = dot_t(g, ob_ref[0]).astype(bf16)
    dh_s[...] = dot_t(g, wo_ref[...]) + dot_t(d_lat, oa_ref[0])

    keep = causal(CHUNK)
    for c in range(rows // CHUNK):
        r = slice(c * CHUNK, (c + 1) * CHUNK)
        b = act_ref[r, INNER : INNER + NSTATE]
        cc = act_ref[r, INNER + NSTATE :]
        b_t = jnp.transpose(b.astype(f32)).astype(bf16)
        masked = jnp.where(keep, dot_t(cc, b), 0.0)
        dt = dt_ref[r, :]
        cum = cum_ref[r, :]
        cum_t = jnp.transpose(cum)
        p_ec = parts_of(jnp.exp(cum))
        p_dt = parts_of(dt)
        p_w = parts_of(jnp.exp(cum[CHUNK - 1 : CHUNK] - cum) * dt)
        for t in range(INNER // TILE):
            cols = slice(t * TILE, (t + 1) * TILE)
            ec = dot(p_ec, expand_ref[:, cols])
            x = act_ref[r, cols].astype(f32)
            xd = (x * dot(p_dt, expand_ref[:, cols])).astype(bf16)
            xw = (x * dot(p_w, expand_ref[:, cols])).astype(bf16)
            state = state_s[:, cols]
            low = state.astype(bf16)
            hc_ref[c, :, cols] = low
            far = dot(cc, low) * ec
            state_s[:, cols] = state * ec[CHUNK - 1 : CHUNK] + dot(b_t, xw)
            for k in range(2):
                head = t * 4 + k * 2
                m1, m2 = (
                    (w * masked).astype(bf16) for w in decayed(cum, cum_t, (head, head + 1), masked)
                )
                pair = split_heads(xd[:, k * LANES : (k + 1) * LANES])
                near = dot(jnp.concatenate([m1, m2], axis=1), pair)
                y_s[r, t * TILE + k * LANES : t * TILE + (k + 1) * LANES] = (
                    near + far[:, k * LANES : (k + 1) * LANES]
                )

    def forward_strip(i, carry):
        r = pl.ds(pl.multiple_of(i * strip, strip), strip)
        total = jnp.zeros((strip, LANES), f32)
        for t in range(INNER // TILE):
            cols = slice(t * TILE, (t + 1) * TILE)
            gate = gate_s[r, cols]
            u = y_s[r, cols] + skip_ref[:, cols] * act_ref[r, cols].astype(f32)
            sig = 1.0 / (1.0 + jnp.exp(-gate))
            silu = gate * sig
            z = u * silu
            square = z * z
            total = total + square[:, :LANES] + square[:, LANES:]
            z_s[r, cols] = z
            gate_s[r, cols] = silu
            prod_s[r, cols] = u * (sig + silu * (1.0 - sig))
        root = lax.rsqrt(jnp.sum(total, -1, keepdims=True) / INNER + epsilon)
        r_s[r, :] = jnp.broadcast_to(root, (strip, LANES))
        for t in range(INNER // TILE):
            cols = slice(t * TILE, (t + 1) * TILE)
            hid_s[r, cols] = (z_s[r, cols] * root * gain_ref[:, cols]).astype(bf16)
        return carry

    lax.fori_loop(0, rows // strip, forward_strip, 0)

    hidden = hid_s[...]
    lat_out = dot(hidden, oa_ref[0]).astype(bf16)
    mixed = dot(hidden, wo_ref[...]) + dot(lat_out, ob_ref[0])
    out_ref[...] = jnp.where(valid, x_ref[0].astype(f32) + mixed, 0.0).astype(bf16)
    tb_ref[...] += dot(jnp.transpose(lat_out.astype(f32)).astype(bf16), g)
    ta_ref[...] += dot(jnp.transpose(d_lat.astype(f32)).astype(bf16), hidden)

    def backward_strip(i, carry):
        r = pl.ds(pl.multiple_of(i * strip, strip), strip)
        total = jnp.zeros((strip, LANES), f32)
        for t in range(INNER // TILE):
            cols = slice(t * TILE, (t + 1) * TILE)
            dh = dh_s[r, cols] * gain_ref[:, cols]
            dh_s[r, cols] = dh
            both = dh * z_s[r, cols]
            total = total + both[:, :LANES] + both[:, LANES:]
        root = r_s[r, 0:1]
        back = jnp.sum(total, -1, keepdims=True) * (root * root * root) / INNER
        for t in range(INNER // TILE):
            cols = slice(t * TILE, (t + 1) * TILE)
            dz = dh_s[r, cols] * root - z_s[r, cols] * back
            dy = (dz * gate_s[r, cols]).astype(bf16)
            dy_ref[r, cols] = dy
            dg_ref[r, cols] = (dz * prod_s[r, cols]).astype(bf16)
            hid_s[r, cols] = (dy.astype(f32) * y_s[r, cols]).astype(bf16)
        return carry

    lax.fori_loop(0, rows // strip, backward_strip, 0)
    rowt_ref[...] = dot_t(hid_s[...], expand_ref[...])

    for c in range(rows // CHUNK):
        r = slice(c * CHUNK, (c + 1) * CHUNK)
        c_t = jnp.transpose(act_ref[r, INNER + NSTATE :].astype(f32)).astype(bf16)
        p_ec = parts_of(jnp.exp(cum_ref[r, :]))
        for t in range(INNER // TILE):
            cols = slice(t * TILE, (t + 1) * TILE)
            ec = dot(p_ec, expand_ref[:, cols])
            scaled = (dy_ref[r, cols].astype(f32) * ec).astype(bf16)
            grad_s[:, cols] += run_s[:, cols] * dot(c_t, scaled)
            run_s[:, cols] = run_s[:, cols] * ec[CHUNK - 1 : CHUNK]

    @pl.when(step == pl.num_programs(0) - 1)
    def _():
        pay_ref[0:NSTATE, :] = grad_s[...].astype(bf16)
        decay = run_s[...]
        high = decay.astype(bf16).astype(f32)
        row = lax.broadcasted_iota(jnp.int32, (RIM, INNER), 0)
        both = jnp.where(row == 0, high, jnp.where(row == 1, decay - high, 0.0))
        pay_ref[NSTATE:, :] = both.astype(bf16)


def middle_call(
    seq, ids, lens, tokens, cotangent, nrm, lat, act, dt, cum, h_in, wg, in_b, wo, out_a, out_b, skip,
    gain, expand,
):
    rows = act.shape[0]
    block = 2 * CHUNK
    steps = rows // block
    by_seq = lambda *shape: pl.BlockSpec((1,) + shape, lambda i, *_: (seq, i, 0))
    by_row = lambda *shape: pl.BlockSpec(shape, lambda i, *_: (i, 0))
    whole = lambda a: pl.BlockSpec(a.shape, lambda i, *_: (0,) * a.ndim)
    chosen = lambda a, width: pl.BlockSpec(
        (1, a.shape[1], width), lambda i, ids, lens: (ids[seq], 0, 0)
    )
    outs = [
        ((rows, DM), bf16),
        ((rows, INNER), bf16),
        ((rows, INNER), bf16),
        ((rows // CHUNK, NSTATE, INNER), bf16),
        ((rows, LANES), f32),
        ((NSTATE + RIM, INNER), bf16),
        ((RANK, DM), f32),
        ((RANK, INNER), f32),
    ]
    return pl.pallas_call(
        functools.partial(middle_kernel, seq=seq),
        grid_spec=pltpu.PrefetchScalarGridSpec(
            num_scalar_prefetch=2,
            grid=(steps,),
            in_specs=[
                by_seq(block, DM),
                by_seq(block, DM),
                by_seq(block, DM),
                by_seq(block, RANK),
                by_row(block, CONV_CH),
                by_row(block, LANES),
                by_row(block, LANES),
                whole(h_in),
                whole(wg),
                chosen(in_b, INNER),
                whole(wo),
                chosen(out_a, RANK),
                chosen(out_b, DM),
                whole(skip),
                whole(gain),
                whole(expand),
            ],
            out_specs=[
                by_row(block, DM),
                by_row(block, INNER),
                by_row(block, INNER),
                pl.BlockSpec((block // CHUNK, NSTATE, INNER), lambda i, *_: (i, 0, 0)),
                by_row(block, LANES),
                pl.BlockSpec((NSTATE + RIM, INNER), lambda i, *_: (0, 0)),
                pl.BlockSpec((RANK, DM), lambda i, *_: (0, 0)),
                pl.BlockSpec((RANK, INNER), lambda i, *_: (0, 0)),
            ],
            scratch_shapes=[
                pltpu.VMEM((block, INNER), f32),
                pltpu.VMEM((block, INNER), f32),
                pltpu.VMEM((block, INNER), f32),
                pltpu.VMEM((block, INNER), f32),
                pltpu.VMEM((block, INNER), bf16),
                pltpu.VMEM((block, LANES), f32),
                pltpu.VMEM((NSTATE, INNER), f32),
                pltpu.VMEM((NSTATE, INNER), f32),
                pltpu.VMEM((1, INNER), f32),
                pltpu.VMEM((block, INNER), f32),
            ],
        ),
        out_shape=[jax.ShapeDtypeStruct(s, d) for s, d in outs],
        compiler_params=pltpu.CompilerParams(vmem_limit_bytes=VMEM_LIMIT),
        name="middle",
    )(ids, lens, tokens, cotangent, nrm, lat, act, dt, cum, h_in, wg, in_b, wo, out_a, out_b, skip, gain, expand)


def scan_back_kernel(
    act_ref, dact_ref, dt_ref, cum_ref, sig_ref, rowt_ref, dy_ref, hc_ref, dh_ref, skip_ref, rate_ref,
    cw_ref, expand_ref, dx_ref, draw_ref, tail_ref, head_ref,
    grad_s, end_s, pre_s,
):
    step = pl.program_id(0)
    rows = act_ref.shape[0]
    keep = causal(CHUNK)
    upper = causal(CHUNK).astype(f32).T
    row = lax.broadcasted_iota(jnp.int32, (CHUNK, LANES), 0)
    lane = lax.broadcasted_iota(jnp.int32, (CHUNK, LANES), 1)

    @pl.when(step == 0)
    def _():
        grad_s[...] = dh_ref[...]
        pre_s[rows : rows + 8, :] = jnp.zeros((8, CONV_CH), f32)

    @pl.when(step > 0)
    def _():
        pre_s[rows : rows + 8, :] = pre_s[0:8, :]

    for c in reversed(range(rows // CHUNK)):
        r = slice(c * CHUNK, (c + 1) * CHUNK)
        b = act_ref[r, INNER : INNER + NSTATE]
        cc = act_ref[r, INNER + NSTATE :]
        b_t = jnp.transpose(b.astype(f32)).astype(bf16)
        c_t = jnp.transpose(cc.astype(f32)).astype(bf16)
        masked = jnp.where(keep, dot_t(cc, b), 0.0)
        dt = dt_ref[r, :]
        cum = cum_ref[r, :]
        cum_t = jnp.transpose(cum)
        p_ec = parts_of(jnp.exp(cum))
        p_dt = parts_of(dt)
        p_w = parts_of(jnp.exp(cum[CHUNK - 1 : CHUNK] - cum))
        d_scores = jnp.zeros((CHUNK, CHUNK), f32)
        d_b = jnp.zeros((CHUNK, NSTATE), f32)
        d_c = jnp.zeros((CHUNK, NSTATE), f32)
        col = jnp.zeros((CHUNK, LANES), f32)
        ends = jnp.zeros((8, LANES), f32)
        for t in range(INNER // TILE):
            cols = slice(t * TILE, (t + 1) * TILE)
            spread = expand_ref[:, cols]
            ec = dot(p_ec, spread)
            dts = dot(p_dt, spread)
            w = dot(p_w, spread)
            x = act_ref[r, cols].astype(f32)
            xd = (x * dts).astype(bf16)
            dy = dy_ref[r, cols]
            dye = (dy.astype(f32) * ec).astype(bf16)
            grad = grad_s[:, cols]
            grad_low = grad.astype(bf16)
            state = hc_ref[c, :, cols]
            far = dot(b, grad_low) * w
            xw = (xd.astype(f32) * w).astype(bf16)
            d_b = d_b + dot_t(xw, grad_low)
            d_c = d_c + dot_t(dye, state)
            out_state = state.astype(f32) * ec[CHUNK - 1 : CHUNK] + dot(b_t, xw)
            end = jnp.sum(grad * out_state, axis=0, keepdims=True)
            end_high = end.astype(bf16)
            end_low = (end - end_high.astype(f32)).astype(bf16)
            ends = ends + dot_t(jnp.broadcast_to(end_high, (8, TILE)), spread)
            ends = ends + dot_t(jnp.broadcast_to(end_low, (8, TILE)), spread)
            grad_s[:, cols] = grad * ec[CHUNK - 1 : CHUNK] + dot(c_t, dye)
            near = []
            for k in range(2):
                head = t * 4 + k * 2
                lanes = slice(k * LANES, (k + 1) * LANES)
                w1, w2 = decayed(cum, cum_t, (head, head + 1), masked)
                both = jnp.concatenate([w1 * masked, w2 * masked], axis=1)
                dy_pair = dy[:, lanes]
                d_both = dot_t(dy_pair, split_heads(xd[:, lanes]))
                d_scores = d_scores + w1 * d_both[:, :CHUNK] + w2 * d_both[:, CHUNK:]
                turned = jnp.transpose(both).astype(bf16)
                two = dot(turned, dy_pair)
                near.append(jnp.where(lane < HDIM, two[:CHUNK], two[CHUNK:]))
            d_xd = jnp.concatenate(near, axis=1) + far
            col = col + dot_t((d_xd * x).astype(bf16), spread)
            d_x = d_xd * dts + skip_ref[:, cols] * dy.astype(f32)
            pre_s[r, cols] = d_x * dact_ref[r, cols].astype(f32)
        d_low = jnp.where(keep, d_scores, 0.0)
        d_c = d_c + dot(d_low.astype(bf16), b)
        d_b = d_b + dot(jnp.transpose(d_low).astype(bf16), cc)
        at_b = slice(INNER, INNER + NSTATE)
        at_c = slice(INNER + NSTATE, CONV_CH)
        pre_s[r, at_b] = d_b * dact_ref[r, at_b].astype(f32)
        pre_s[r, at_c] = d_c * dact_ref[r, at_c].astype(f32)
        d_cum = rowt_ref[r, :] - dt * col
        d_cum = d_cum + jnp.where(row == CHUNK - 1, ends[0:1], 0.0)
        d_log = dot_precise(upper, d_cum)
        d_raw = (d_log * rate_ref[...] + col) * sig_ref[r, :]
        draw_ref[r, :] = jnp.where(lane < HEADS, d_raw, 0.0).astype(bf16)

    strip = 64
    for t in range(CONV_CH // TILE):
        cols = slice(t * TILE, (t + 1) * TILE)
        weights = [cw_ref[j : j + 1, cols] for j in range(4)]
        for i in range(rows // strip):
            at = i * strip
            total = weights[3] * pre_s[at : at + strip, cols]
            for j in range(3):
                total = total + weights[j] * pre_s[at + 3 - j : at + 3 - j + strip, cols]
            dx_ref[at : at + strip, cols] = total.astype(bf16)
            if i == rows // strip - 1:
                end = total[strip - RIM :, :]

                @pl.when(step == 0)
                def _(end=end, cols=cols):
                    tail_ref[:, cols] = end

    @pl.when(step == pl.num_programs(0) - 1)
    def _():
        head_ref[...] = pre_s[0:RIM, :].astype(bf16)


def scan_back_call(act, dact, dt, cum, sig, rowt, dy, hc, dh, skip, rate, conv_w, expand):
    rows = act.shape[0]
    block = 2 * CHUNK
    steps = rows // block
    by_row = lambda *shape: pl.BlockSpec(shape, lambda i: (steps - 1 - i, 0))
    whole = lambda a: pl.BlockSpec(a.shape, lambda i: (0,) * a.ndim)
    outs = [
        ((rows, CONV_CH), bf16),
        ((rows, LANES), bf16),
        ((RIM, CONV_CH), f32),
        ((RIM, CONV_CH), bf16),
    ]
    return pl.pallas_call(
        scan_back_kernel,
        grid=(steps,),
        in_specs=[
            by_row(block, CONV_CH),
            by_row(block, CONV_CH),
            by_row(block, LANES),
            by_row(block, LANES),
            by_row(block, LANES),
            by_row(block, LANES),
            by_row(block, INNER),
            pl.BlockSpec((block // CHUNK, NSTATE, INNER), lambda i: (steps - 1 - i, 0, 0)),
            whole(dh),
            whole(skip),
            whole(rate),
            whole(conv_w),
            whole(expand),
        ],
        out_specs=[
            by_row(block, CONV_CH),
            by_row(block, LANES),
            pl.BlockSpec((RIM, CONV_CH), lambda i: (0, 0)),
            pl.BlockSpec((RIM, CONV_CH), lambda i: (0, 0)),
        ],
        scratch_shapes=[
            pltpu.VMEM((NSTATE, INNER), f32),
            pltpu.VMEM((8, INNER), f32),
            pltpu.VMEM((block + 8, CONV_CH), f32),
        ],
        out_shape=[jax.ShapeDtypeStruct(s, d) for s, d in outs],
        compiler_params=pltpu.CompilerParams(vmem_limit_bytes=VMEM_LIMIT),
        name="scan_back",
    )(act, dact, dt, cum, sig, rowt, dy, hc, dh, skip, rate, conv_w, expand)


def input_back_kernel(
    ids, lens, x_ref, cot_ref, nrm_ref, lat_ref, dg_ref, dx_ref, draw_ref, tail_ref, next_ref, cw_ref,
    wg_ref, wx_ref, wdt_ref, ia_ref, ib_ref, gain_ref, out_ref, tb_ref, ta_ref, dx_s, dn_s, *, seq,
):
    rows = dx_ref.shape[0]
    dx_s[...] = dx_ref[...]
    row = lax.broadcasted_iota(jnp.int32, (RIM, CONV_CH), 0)
    later = next_ref[...].astype(f32)
    total = tail_ref[...]
    for back in range(1, 4):
        term = jnp.zeros((1, CONV_CH), f32)
        for j in range(0, 4 - back):
            term = term + cw_ref[j : j + 1, :] * later[3 - back - j : 4 - back - j, :]
        total = total + jnp.where(row == RIM - back, term, 0.0)
    dx_s[rows - RIM :, :] = total.astype(bf16)
    d_gate = dg_ref[...]
    d_xbc = dx_s[...]
    d_x = dx_s[:, :INNER]
    d_lat = (dot_t(d_gate, ib_ref[0, :, :INNER]) + dot_t(d_x, ib_ref[0, :, INNER:])).astype(bf16)
    lat_t = jnp.transpose(lat_ref[0].astype(f32)).astype(bf16)
    tb_ref[:, :INNER] = dot(lat_t, d_gate)
    tb_ref[:, INNER:] = dot(lat_t, d_x)
    ta_ref[...] = dot(jnp.transpose(d_lat.astype(f32)).astype(bf16), nrm_ref[0])
    dn_s[...] = (
        dot_t(d_gate, wg_ref[...])
        + dot_t(d_xbc, wx_ref[...])
        + dot_t(draw_ref[...], wdt_ref[...])
        + dot_t(d_lat, ia_ref[0])
    )
    strip = 32

    def body(i, carry):
        r = pl.ds(pl.multiple_of(i * strip, strip), strip)
        x = x_ref[0, r, :].astype(f32)
        root = lax.rsqrt(jnp.mean(x * x, -1, keepdims=True) + epsilon)
        dn = dn_s[r, :] * gain_ref[...]
        back = jnp.mean(dn * x, -1, keepdims=True) * (root * root * root)
        position = i * strip + lax.broadcasted_iota(jnp.int32, (strip, 1), 0)
        kept = jnp.where(position < lens[seq], cot_ref[0, r, :].astype(f32), 0.0)
        out_ref[r, :] = dn * root - x * back + kept
        return carry

    lax.fori_loop(0, rows // strip, body, 0)


def input_back_call(
    seq, ids, lens, tokens, cotangent, nrm, lat, dg, dx, draw, tail, later, conv_w, wg, wx, wdt, in_a, in_b, gain
):
    rows = dx.shape[0]
    by_seq = lambda *shape: pl.BlockSpec((1,) + shape, lambda i, *_: (seq, 0, 0))
    whole = lambda a: pl.BlockSpec(a.shape, lambda i, *_: (0,) * a.ndim)
    chosen = lambda a: pl.BlockSpec((1,) + a.shape[1:], lambda i, ids, lens: (ids[seq], 0, 0))
    outs = [((rows, DM), f32), ((RANK, ZX), f32), ((RANK, DM), f32)]
    return pl.pallas_call(
        functools.partial(input_back_kernel, seq=seq),
        grid_spec=pltpu.PrefetchScalarGridSpec(
            num_scalar_prefetch=2,
            grid=(1,),
            in_specs=[
                by_seq(rows, DM),
                by_seq(rows, DM),
                by_seq(rows, DM),
                by_seq(rows, RANK),
                whole(dg),
                whole(dx),
                whole(draw),
                whole(tail),
                whole(later),
                whole(conv_w),
                whole(wg),
                whole(wx),
                whole(wdt),
                chosen(in_a),
                chosen(in_b),
                whole(gain),
            ],
            out_specs=[pl.BlockSpec(s, lambda i, *_: (0, 0)) for s, _ in outs],
            scratch_shapes=[pltpu.VMEM((rows, CONV_CH), bf16), pltpu.VMEM((rows, DM), f32)],
        ),
        out_shape=[jax.ShapeDtypeStruct(s, d) for s, d in outs],
        compiler_params=pltpu.CompilerParams(vmem_limit_bytes=VMEM_LIMIT),
        name="input_back",
    )(ids, lens, tokens, cotangent, nrm, lat, dg, dx, draw, tail, later, conv_w, wg, wx, wdt, in_a, in_b, gain)


def shifted(value, axis, steps):
    count = lax.axis_size(axis)
    pairs = [(i, i + steps) for i in range(count) if 0 <= i + steps < count]
    return lax.ppermute(value, axis, pairs)


def swapped(value, axis, bit):
    return lax.ppermute(value, axis, [(i, i ^ bit) for i in range(lax.axis_size(axis))])


def unpacked(payload):
    state = payload[:NSTATE].astype(f32)
    decay = payload[NSTATE : NSTATE + 1].astype(f32) + payload[NSTATE + 1 : NSTATE + 2].astype(f32)
    return state, decay


def packed(state, decay):
    high = decay.astype(bf16)
    low = (decay - high.astype(f32)).astype(bf16)
    rest = jnp.zeros((RIM - 2, INNER), bf16)
    return jnp.concatenate([state.astype(bf16), high, low, rest], axis=0)


def joined(first, second):
    return second[1] * first[0] + second[0], first[1] * second[1]


def entering(payload, reverse):
    count = lax.axis_size("ctx")
    place = lax.axis_index("ctx")
    sign = -1 if reverse else 1
    late = (place % 2 == 0) if reverse else (place % 2 == 1)
    own = unpacked(payload)
    other = unpacked(swapped(payload, "ctx", 1))
    first = jax.tree.map(lambda a, b: jnp.where(late, a, b), other, own)
    second = jax.tree.map(lambda a, b: jnp.where(late, a, b), own, other)
    both = joined(first, second)
    chips = count // 2
    before = unpacked(shifted(packed(*both), "ctx", 2 * sign))
    step, run = 1, None
    while 2 * step < chips + 1 and step * 2 < chips:
        run = joined(before, both) if run is None else run
        far = unpacked(shifted(packed(*run), "ctx", 4 * step * sign))
        before = joined(far, before)
        run = joined(far, run)
        step *= 2
    return jnp.where(late, other[1] * before[0] + other[0], before[0])


def shards(
    tokens, cotangent, lengths, adapter_ids, norm_gain, w_in, conv_weight, conv_bias, dt_bias, a_log,
    skip_scale, inner_gain, w_out, in_a, in_b, out_a, out_b,
):
    seqs, slots, _ = tokens.shape
    owners = lax.axis_size("dp")
    ids = adapter_ids
    lens = jnp.clip(lengths - lax.axis_index("ctx") * slots, 0, slots).astype(jnp.int32)

    def grouped(row):
        padded = jnp.pad(row.reshape(-1, HEADS), ((0, 0), (0, GROUP - HEADS)))
        return jnp.tile(padded, (1, LANES // GROUP))

    rate = grouped(-jnp.exp(a_log))
    dtb = grouped(dt_bias)
    lane = jnp.arange(LANES)[:, None]
    head = jnp.arange(INNER)[None, :] // HDIM
    expand = ((lane % GROUP == head) & (lane < 3 * GROUP)).astype(bf16)
    skip = jnp.repeat(skip_scale, HDIM)[None, :]
    gain = inner_gain[None, :]
    n_gain = norm_gain[None, :]
    conv_b = conv_bias[None, :]

    gate_cols, rest = w_in[:, :INNER], w_in[:, INNER:]
    rest = jnp.pad(rest, ((0, 0), (0, 15 * LANES - rest.shape[1])))
    full_rest = lax.all_gather(rest, "dp", axis=0, tiled=True)
    full_gate = lax.all_gather(gate_cols, "dp", axis=0, tiled=True)
    full_out = lax.all_gather(w_out, "dp", axis=0, tiled=True)
    wx = full_rest[:, :CONV_CH]
    wdt = grouped(full_rest[:, CONV_CH : CONV_CH + HEADS])

    rim = shifted(tokens[:, slots - RIM :], "ctx", 1)
    nrm, nrim, lat, lrim = norm_call(ids, tokens, rim, n_gain, in_a)
    fronts = [
        front_call(s, ids, nrm, nrim, lat, lrim, wx, wdt, in_b, conv_weight, conv_b, dtb, rate, expand)
        for s in range(seqs)
    ]
    states = [entering(front[5], False) for front in fronts]
    middles = [
        middle_call(
            s, ids, lens, tokens, cotangent, nrm, lat, fronts[s][0], fronts[s][2], fronts[s][3], states[s],
            full_gate, in_b, full_out, out_a, out_b, skip, gain, expand,
        )
        for s in range(seqs)
    ]
    grads = [entering(mid[5], True) for mid in middles]
    backs = []
    for s in range(seqs):
        act, dact, dt, cum, sig, _ = fronts[s]
        _, dy, _, hc, rowt, _, _, _ = middles[s]
        backs.append(
            scan_back_call(act, dact, dt, cum, sig, rowt, dy, hc, grads[s], skip, rate, conv_weight, expand)
        )
    nexts = [shifted(back[3], "ctx", -1) for back in backs]
    lasts = [
        input_back_call(
            s, ids, lens, tokens, cotangent, nrm, lat, middles[s][2], backs[s][0], backs[s][1], backs[s][2],
            nexts[s], conv_weight, full_gate, wx, wdt, in_a, in_b, n_gain,
        )
        for s in range(seqs)
    ]

    def by_owner(terms):
        stacked = jnp.stack(terms)
        return stacked.reshape(seqs, RANK, owners, -1).transpose(2, 0, 1, 3)

    kinds = (
        [last[2] for last in lasts],
        [last[1] for last in lasts],
        [mid[7] for mid in middles],
        [mid[6] for mid in middles],
    )
    pieces = [by_owner(terms) for terms in kinds]
    widths = [piece.shape[-1] for piece in pieces]
    sent = jnp.concatenate(pieces, axis=-1).astype(bf16)
    got = lax.all_to_all(sent, "dp", 0, 0)
    every = lax.all_gather(adapter_ids, "dp", axis=0, tiled=True)
    chosen = (every[None, :] == jnp.arange(in_a.shape[0])[:, None]).astype(f32)
    flat = got.reshape(owners * seqs, -1).astype(f32)
    mine = jnp.sum(chosen[:, :, None] * flat[None], axis=1)
    bit = 1
    while bit < lax.axis_size("ctx"):
        mine = mine + swapped(mine, "ctx", bit)
        bit *= 2
    mine = mine.reshape(in_a.shape[0], RANK, -1)
    cuts = [sum(widths[:k]) for k in range(5)]
    g_ia, g_ib, g_oa, g_ob = (mine[:, :, cuts[k] : cuts[k + 1]] for k in range(4))
    return (
        jnp.stack([mid[0] for mid in middles]),
        jnp.stack([last[0] for last in lasts]),
        jnp.swapaxes(g_ia, 1, 2),
        g_ib,
        jnp.swapaxes(g_oa, 1, 2),
        g_ob,
    )


def solution(mesh):
    split = P("dp", "ctx", None)
    return jax.shard_map(
        shards,
        mesh=mesh,
        in_specs=(
            split, split, P("dp"), P("dp"), P(), P("dp", None), P(), P(), P(), P(), P(), P(),
            P("dp", None), P(), P(), P(), P(),
        ),
        out_specs=(
            split, split, P(None, "dp", None), P(None, None, "dp"), P(None, "dp", None), P(None, None, "dp"),
        ),
        check_vma=False,
    )
```

time: 984 us -> 404 us (0.41)
  matrix products: 254 us -> 0 us
  waiting for transfers between devices: 332 us -> 135 us
  Pallas kernels: 0 us -> 165 us
  other arithmetic: 184 us -> 21.5 us
  local copies, waits for them, and re-layouts: 162 us -> 24.5 us
  starting transfers between devices: 9.83 us -> 23.4 us
    dot_general x64 -> x0, matrix products: 254 us -> none  [the longest x6 92.1 us: block_outputs(): inside = jnp.einsum('chqs,cshp->cqhp', weights, x_blocks, precision=precise)]
    pallas_call x0 -> x9, Pallas kernels: none -> 165 us  [the longest x2 64 us: middle_call(): pl.pallas_call(functools.partial(middle_kernel, seq=seq), grid_spec=pltpu...]
    unnamed x15 -> x3, waiting for transfers between devices: 81.9 us -> 0.73 us
    psum x2 -> x0, waiting for transfers between devices: 65.1 us -> none  [shards(): lax.psum((gradients[0], gradients[1], gradients[2], gradients[3]), 'ctx')]
    reduce_scatter x1 -> x0, waiting for transfers between devices: 61.7 us -> none  [shards(): lax.psum_scatter(summed[1], 'dp', scatter_dimension=2, tiled=True)]
    unnamed x509 -> x61, local copies, waits for them, and re-layouts: 68.6 us -> 9.88 us
    another operation x25 -> x10, other arithmetic: 55.3 us -> 6.67 us
    ppermute x4 -> x13, waiting for transfers between devices: 0.32 us -> 37.2 us  [the longest x7 27 us: shifted(): return lax.ppermute(value, axis, pairs)]
  transfers between devices with their start and end apart: 16 -> 17, of which waited for: 9 -> 9; matrix products, arithmetic and copies ran while one was open for 30% -> 8% of each run, Pallas kernels for 0% -> 22%
where the time goes in v1:
time: 404 us; the launch traced here: 396 us
  Pallas kernels  165 us (41%)
  waiting for transfers between devices  135 us (33%)
  local copies, waits for them, and re-layouts  24.5 us (6%)
  starting transfers between devices  23.4 us (6%)
  other arithmetic  21.5 us (5%)
  between operations  15.4 us (4%)
  blocking collectives  11.9 us (3%)
    pallas_call x2, Pallas kernels, middle_call(): pl.pallas_call(functools.partial(middle_kernel, seq=seq), grid_spec=pltpu...  64 us
    all_gather x1, waiting for transfers between devices, shards(): full_gate = lax.all_gather(gate_cols, 'dp', axis=0, tiled=True)  48.9 us
    all_gather x1, waiting for transfers between devices, shards(): full_rest = lax.all_gather(rest, 'dp', axis=0, tiled=True)  47.8 us
    pallas_call x2, Pallas kernels, scan_back_call(): pl.pallas_call(scan_back_kernel, grid=(steps,), in_specs=[by_row(block, C...  39.2 us
    pallas_call x2, Pallas kernels, front_call(): pl.pallas_call(front_kernel, grid_spec=pltpu.PrefetchScalarGridSpec(num_s...  30 us
    ppermute x7, waiting for transfers between devices, shifted(): return lax.ppermute(value, axis, pairs)  27 us
    pallas_call x2, Pallas kernels, input_back_call(): pl.pallas_call(functools.partial(input_back_kernel, seq=seq), grid_spec=p...  26.8 us
    ppermute x7, starting transfers between devices, shifted(): return lax.ppermute(value, axis, pairs)  15.7 us
  transfers between devices with their start and end apart: 17, of which 9 were waited for; matrix products, arithmetic and copies ran while one was open for 8% of the time, Pallas kernels for 22%

profile of v1, /device:TPU:0, one launch (start us, length us, event | category | flops | bytes accessed | tf_op | source)
XLA Modules:
  0.0 396.4 jit_solution(15353215702750065540)
XLA Ops:
  7.3 1.1 slice.112
  8.3 0.8 pad.15
  9.2 0.7 all-gather.8.cloned.1.call-update
  9.9 0.8 slice.111
  10.7 2.3 collective-permute-start
  13.2 1.0 and_convert_fusion.expand_ref
  14.1 0.7 tile.38.rate_ref
  14.8 0.6 tile.35.dtb_ref
  16.6 1.5 copy.46.a_ref.ia_ref
  18.1 0.6 copy-done.14
  18.7 5.4 %norm.1 = (bf16[2,512,768]{2,1,0:T(8,128)(2,1)}, bf16[2,16,768]{2,1,0:T(8,128)(2,1)}, bf16[2,512,16]{2,1,0:T(8,128)(2,1)}, bf16[2,16,16]{2,1,0:T(8,128)(2,1)}) custom-call(s32[2]{0:T(128)} %ids.13, bf16[2,512,768]{2,1,0:T(8,128)(2,1)} %x_ref.9, bf16[2,16,768]{2,1,0:T(8,128)(2,1)} %copy-done.14, f32[1,768]{1,0:T(1,128)} %broadcast_in_dim.8.gain_ref, ...), custom_call_target="tpu_custom_call" | custom-call | tf_op jit(solution)/shard_map/norm/pallas_call | solution.py:88
  24.1 47.8 %all-gather.4.cloned.1.call-done = bf16[768,1920]{1,0:T(8,128)(2,1)} async-done(((bf16[96,1920]{1,0:T(8,128)(2,1)}), bf16[768,1920]{1,0:T(8,128)(2,1)}) %all-gather.4.cloned.1.call-update) | async-done | bytes 2949136 | tf_op jit(solution)/shard_map/all_gather | solution.py:770
  71.9 0.9 slice.149
  73.0 0.8 copy.48.wdt_ref
  73.8 3.5 slice.148.wx_ref
  77.3 15.0 %front.2 = (bf16[512,1792]{1,0:T(8,128)(2,1)}, bf16[512,1792]{1,0:T(8,128)(2,1)}, f32[512,128]{1,0:T(8,128)}, f32[512,128]{1,0:T(8,128)}, f32[512,128]{1,0:T(8,128)}, /*index=5*/bf16[144,1536]{1,0:T(8,128)(2,1)}) custom-call(s32[2]{0:T(128)} %ids.13, bf16[2,512,768]{2,1,0:T(8,128)(2,1)} %get-tuple-element.52.nrm_ref, ...), custom_call_target="tpu_custom_call" | custom-call | tf_op jit(solution)/shard_map/front/pallas_call | solution.py:190
  92.3 1.7 slice.122
  94.8 0.7 broadcast_in_dim_reshape.3.skip_ref
  95.5 2.7 copy.49.oa_ref
  98.8 14.9 %front.3 = (bf16[512,1792]{1,0:T(8,128)(2,1)}, bf16[512,1792]{1,0:T(8,128)(2,1)}, f32[512,128]{1,0:T(8,128)}, f32[512,128]{1,0:T(8,128)}, f32[512,128]{1,0:T(8,128)}, /*index=5*/bf16[144,1536]{1,0:T(8,128)(2,1)}) custom-call(s32[2]{0:T(128)} %ids.13, bf16[2,512,768]{2,1,0:T(8,128)(2,1)} %get-tuple-element.52.nrm_ref, ...), custom_call_target="tpu_custom_call" | custom-call | tf_op jit(solution)/shard_map/front/pallas_call | solution.py:190
  114.6 3.7 collective-permute-start.2
  118.6 9.2 %collective-permute-done.2 = bf16[144,1536]{1,0:T(8,128)(2,1)S(1)} collective-permute-done((bf16[144,1536]{1,0:T(8,128)(2,1)S(1)}, bf16[144,1536]{1,0:T(8,128)(2,1)S(1)}, u32[]{:S(2)}, u32[]{:S(2)}) %collective-permute-start.2) | collective-permute-done | bytes 442400 | tf_op jit(solution)/shard_map/ppermute | solution.py:699
  127.7 1.1 convert_select_fusion.11.h_ref
  128.8 48.9 %all-gather.6.cloned.1.call-done.wg_ref = bf16[768,1536]{1,0:T(8,128)(2,1)} async-done(((bf16[96,1536]{1,0:T(8,128)(2,1)}), bf16[768,1536]{1,0:T(8,128)(2,1)}) %all-gather.6.cloned.1.call-update) | async-done | bytes 2359312 | tf_op jit(solution)/shard_map/all_gather | solution.py:771
  177.7 31.9 %middle.2 = (bf16[512,768]{1,0:T(8,128)(2,1)}, bf16[512,1536]{1,0:T(8,128)(2,1)}, bf16[512,1536]{1,0:T(8,128)(2,1)}, bf16[4,128,1536]{2,1,0:T(8,128)(2,1)}, f32[...) custom-call(s32[2]{0:T(128)} %ids.13, s32[2]{0:T(128)} %subtract_clamp_fusion.lens, ...), custom_call_target="tpu_custom_call" | custom-call | tf_op jit(solution)/shard_map/middle/pallas_call | solution.py:398
  209.7 2.0 collective-permute-done.5
  211.6 0.9 fusion.28
  212.5 0.8 fusion.33
  213.3 1.2 fusion.8
  214.8 3.7 collective-permute-start.4
  218.5 9.4 %collective-permute-done.4 = bf16[144,1536]{1,0:T(8,128)(2,1)S(1)} collective-permute-done((bf16[144,1536]{1,0:T(8,128)(2,1)S(1)}, bf16[144,1536]{1,0:T(8,128)(2,1)S(1)}, u32[]{:S(2)}, u32[]{:S(2)}) %collective-permute-start.4) | collective-permute-done | bytes 442400 | tf_op jit(solution)/shard_map/ppermute | solution.py:699
  227.9 1.0 convert_select_fusion.10.h_ref
  228.9 32.1 %middle.3 = (bf16[512,768]{1,0:T(8,128)(2,1)}, bf16[512,1536]{1,0:T(8,128)(2,1)}, bf16[512,1536]{1,0:T(8,128)(2,1)}, bf16[4,128,1536]{2,1,0:T(8,128)(2,1)}, f32[...) custom-call(s32[2]{0:T(128)} %ids.13, s32[2]{0:T(128)} %subtract_clamp_fusion.lens, ...), custom_call_target="tpu_custom_call" | custom-call | tf_op jit(solution)/shard_map/middle/pallas_call | solution.py:398
  261.4 1.3 collective-permute-start.6
  263.1 0.9 fusion.29
  264.0 0.8 fusion.36
  264.8 1.2 fusion.11
  266.1 1.8 collective-permute-start.9
  267.9 8.4 %collective-permute-done.6 = bf16[144,1536]{1,0:T(8,128)(2,1)S(1)} collective-permute-done((bf16[144,1536]{1,0:T(8,128)(2,1)S(1)}, bf16[144,1536]{1,0:T(8,128)(2,1)S(1)}, u32[]{:S(2)}, u32[]{:S(2)}) %collective-permute-start.6) | collective-permute-done | bytes 442400 | tf_op jit(solution)/shard_map/ppermute | solution.py:699
  276.3 1.0 convert_select_fusion.9.dh_ref
  277.3 19.6 %scan_back.2 = (bf16[512,1792]{1,0:T(8,128)(2,1)}, bf16[512,128]{1,0:T(8,128)(2,1)}, f32[16,1792]{1,0:T(8,128)}, bf16[16,1792]{1,0:T(8,128)(2,1)}) custom-call(bf16[512,1792]{1,0:T(8,128)(2,1)} %get-tuple-element.56.act_ref, bf16[512,1792]{1,0:T(8,128)(2,1)} %get-tuple-element.67.dact_ref, f32[512,128]{1,0:T(8,128)} %get-tuple-element.57.dt_ref, ...), custom_call_target="tpu_custom_call" | custom-call | tf_op jit(solution)/shard_map/scan_back/pallas_call | solution.py:576
  296.9 1.5 collective-permute-start.7
  298.5 1.0 convert_select_fusion.8.dh_ref
  299.6 19.6 %scan_back.3 = (bf16[512,1792]{1,0:T(8,128)(2,1)}, bf16[512,128]{1,0:T(8,128)(2,1)}, f32[16,1792]{1,0:T(8,128)}, bf16[16,1792]{1,0:T(8,128)(2,1)}) custom-call(bf16[512,1792]{1,0:T(8,128)(2,1)} %get-tuple-element.61.act_ref, bf16[512,1792]{1,0:T(8,128)(2,1)} %get-tuple-element.79.dact_ref, f32[512,128]{1,0:T(8,128)} %get-tuple-element.62.dt_ref, ...), custom_call_target="tpu_custom_call" | custom-call | tf_op jit(solution)/shard_map/scan_back/pallas_call | solution.py:576
  319.2 1.5 collective-permute-start.10
  321.5 13.4 %input_back.2 = (f32[512,768]{1,0:T(8,128)}, f32[16,3072]{1,0:T(8,128)}, f32[16,768]{1,0:T(8,128)}) custom-call(s32[2]{0:T(128)} %ids.13, s32[2]{0:T(128)} %subtract_clamp_fusion.lens, bf16[2,512,768]{2,1,0:T(8,128)(2,1)} %x_ref.9, bf16[2,512,768]{2,1,0:T(8,128)(2,1)} %cot_ref.7, bf16[2,512,768]{2,1,0:T(8,128)(2,1)} %get-tuple-element.52.nrm_ref, ...), custom_call_target="tpu_custom_call" | custom-call | tf_op jit(solution)/shard_map/input_back/pallas_call | solution.py:664
  334.9 0.8 convert.41
  335.8 0.9 convert.43
  337.4 13.4 %input_back.3 = (f32[512,768]{1,0:T(8,128)}, f32[16,3072]{1,0:T(8,128)}, f32[16,768]{1,0:T(8,128)}) custom-call(s32[2]{0:T(128)} %ids.13, s32[2]{0:T(128)} %subtract_clamp_fusion.lens, bf16[2,512,768]{2,1,0:T(8,128)(2,1)} %x_ref.9, bf16[2,512,768]{2,1,0:T(8,128)(2,1)} %cot_ref.7, bf16[2,512,768]{2,1,0:T(8,128)(2,1)} %get-tuple-element.52.nrm_ref, ...), custom_call_target="tpu_custom_call" | custom-call | tf_op jit(solution)/shard_map/input_back/pallas_call | solution.py:664
  350.8 0.8 convert.42
  351.7 0.9 convert.44
  352.8 1.0 pad_maximum_fusion.2
  353.8 3.5 all-to-all-start
  358.8 11.9 %all-reduce.4 = s32[16]{0:T(128)S(1)} all-reduce(s32[16]{0:T(128)S(1)} %dynamic-update-slice), channel_id=1, replica_groups=mesh['dp'=8,'ctx'=4] {'dp'}, use_global_device_ids=true, to_apply=%add.4 | all-reduce | flops 16 | bytes 128
  370.8 1.2 multiply_reduce_fusion
  372.1 1.6 collective-permute-done.11
  373.8 3.3 collective-permute-start.12
  377.1 1.3 pad_maximum_fusion.1
  378.4 1.9 pad_maximum_fusion
  380.3 6.3 %collective-permute-done.12 = f32[8,12288]{1,0:T(8,128)S(1)} collective-permute-done((f32[8,12288]{1,0:T(8,128)S(1)}, f32[8,12288]{1,0:T(8,128)S(1)}, u32[]{:S(2)}, u32[]{:S(2)}) %collective-permute-start.12) | collective-permute-done | bytes 393248 | tf_op jit(solution)/shard_map/ppermute | solution.py:703
  386.9 0.7 copy.78
  387.6 0.7 copy.69
  388.3 0.6 copy.71
  389.0 0.6 copy.79
  (130 shorter events, 8.6 us)
Async XLA Ops:
  7.2 6.0 %copy-start.20 = (f32[24]{0:T(128)S(1)}, f32[24]{0:T(128)}, u32[]{:S(2)}) copy-start(f32[24]{0:T(128)} %param.25) | copy-start | bytes 292
  7.2 6.0 %copy-start.21 = (f32[24]{0:T(128)S(1)}, f32[24]{0:T(128)}, u32[]{:S(2)}) copy-start(f32[24]{0:T(128)} %param.26) | copy-start | bytes 292
  7.2 8.3 %copy-start.18 = (f32[768]{0:T(1024)S(1)}, f32[768]{0:T(1024)}, u32[]{:S(2)}) copy-start(f32[768]{0:T(1024)} %param.21) | copy-start | bytes 9220
  7.2 8.8 %copy-start.17 = (f32[1792]{0:T(1024)S(1)}, f32[1792]{0:T(1024)}, u32[]{:S(2)}) copy-start(f32[1792]{0:T(1024)} %param.24) | copy-start | bytes 21508
  7.2 9.4 %copy-start.7 = (bf16[8,768,16]{1,2,0:T(8,128)(2,1)S(1)}, bf16[8,768,16]{1,2,0:T(8,128)(2,1)}, u32[]{:S(2)}) copy-start(bf16[8,768,16]{1,2,0:T(8,128)(2,1)} %param.30) | copy-start | bytes 589828
  7.2 64.7 %all-gather.4.cloned.1.call-start = ((), (), s32[]{:S(2)}) async-start(), calls=%async_computation.1 | async-start | bytes 3317760 | tf_op jit(solution)/shard_map/all_gather | solution.py:770
  9.1 119.7 %all-gather.8.cloned.1.call-start = ((), (), s32[]{:S(2)}) async-start(), calls=%async_computation.3 | async-start | bytes 2654208 | tf_op jit(solution)/shard_map/all_gather | solution.py:772
  9.9 167.8 %all-gather.6.cloned.1.call-start = ((), (), s32[]{:S(2)}) async-start(), calls=%async_computation.2 | async-start | bytes 2654208 | tf_op jit(solution)/shard_map/all_gather | solution.py:771
  10.7 7.4 %collective-permute-start = (bf16[2,16,768]{2,1,0:T(8,128)(2,1)S(1)}, bf16[2,16,768]{2,1,0:T(8,128)(2,1)S(1)}, u32[]{:S(2)}, u32[]{:S(2)}) collective-permute-start(bf16[2,16,768]{2,1,0:T(8,128)(2,1)S(1)} %slice.111), channel_id=1, source_target_pairs={{0,1},{1,2},{2,3},{4,5},{5,6},{6,7},{8,9},{9,10},{10,11},{12,13},{... | collective-permute-start | bytes 147464 | tf_op jit(solution)/shard_map/ppermute | solution.py:699
  18.1 0.6 copy-start.14
  77.3 16.8 %copy-start.16 = (f32[1536]{0:T(1024)S(1)}, f32[1536]{0:T(1024)}, u32[]{:S(2)}) copy-start(f32[1536]{0:T(1024)} %param.28) | copy-start | bytes 18436
  77.3 17.4 %copy-start.19 = (f32[24]{0:T(128)S(1)}, f32[24]{0:T(128)}, u32[]{:S(2)}) copy-start(f32[24]{0:T(128)} %param.27) | copy-start | bytes 292
  77.3 18.2 %copy-start.6 = (bf16[8,1536,16]{1,2,0:T(8,128)(2,1)S(1)}, bf16[8,1536,16]{1,2,0:T(8,128)(2,1)}, u32[]{:S(2)}) copy-start(bf16[8,1536,16]{1,2,0:T(8,128)(2,1)} %param.32) | copy-start | bytes 1179652
  92.3 21.8 %collective-permute-start.1 = (bf16[144,1536]{1,0:T(8,128)(2,1)}, bf16[144,1536]{1,0:T(8,128)(2,1)S(1)}, u32[]{:S(2)}, u32[]{:S(2)}) collective-permute-start(bf16[144,1536]{1,0:T(8,128)(2,1)} %get-tuple-element.59), channel_id=1, source_target_pairs={{0,1},{1,0},{2,3},{3,2},{4,5},{5,4},{6,7},{7,6},{8,9},{9,8},{10,11... | collective-permute-start | bytes 1327112 | tf_op jit(solution)/shard_map/ppermute | solution.py:703
  94.1 4.1 %copy-start.22 = (s32[2]{0:T(128)S(1)}, s32[2]{0:T(128)}, u32[]{:S(2)}) copy-start(s32[2]{0:T(128)} %param.19) | copy-start | bytes 28
  98.8 15.4 %copy-start.4 = (bf16[144,1536]{1,0:T(8,128)(2,1)S(1)}, bf16[144,1536]{1,0:T(8,128)(2,1)}, u32[]{:S(2)}) copy-start(bf16[144,1536]{1,0:T(8,128)(2,1)} %get-tuple-element.59) | copy-start | bytes 1327108
  113.7 4.6 %copy-start.5 = (bf16[144,1536]{1,0:T(8,128)(2,1)S(1)}, bf16[144,1536]{1,0:T(8,128)(2,1)}, u32[]{:S(2)}) copy-start(bf16[144,1536]{1,0:T(8,128)(2,1)} %get-tuple-element.64) | copy-start | bytes 1327108
  113.7 4.6 %collective-permute-start.3 = (bf16[144,1536]{1,0:T(8,128)(2,1)}, bf16[144,1536]{1,0:T(8,128)(2,1)S(1)}, u32[]{:S(2)}, u32[]{:S(2)}) collective-permute-start(bf16[144,1536]{1,0:T(8,128)(2,1)} %get-tuple-element.64), channel_id=1, source_target_pairs={{0,1},{1,0},{2,3},{3,2},{4,5},{5,4},{6,7},{7,6},{8,9},{9,8},{10,11... | collective-permute-start | bytes 1327112 | tf_op jit(solution)/shard_map/ppermute | solution.py:703
  114.6 13.1 %collective-permute-start.2 = (bf16[144,1536]{1,0:T(8,128)(2,1)S(1)}, bf16[144,1536]{1,0:T(8,128)(2,1)S(1)}, u32[]{:S(2)}, u32[]{:S(2)}) collective-permute-start(bf16[144,1536]{1,0:T(8,128)(2,1)S(1)} %maximum_maximum_fusion), channel_id=1, source_target_pairs={{0,2},{1,3},{4,6},{5,7},{8,10},{9,11},{12,14},{13,15},{16,18},{17,... | collective-permute-start | bytes 1327112 | tf_op jit(solution)/shard_map/ppermute | solution.py:699
  209.6 2.1 collective-permute-start.5
  214.8 13.1 %collective-permute-start.4 = (bf16[144,1536]{1,0:T(8,128)(2,1)S(1)}, bf16[144,1536]{1,0:T(8,128)(2,1)S(1)}, u32[]{:S(2)}, u32[]{:S(2)}) collective-permute-start(bf16[144,1536]{1,0:T(8,128)(2,1)S(1)} %get-tuple-element.121), channel_id=1, source_target_pairs={{0,2},{1,3},{4,6},{5,7},{8,10},{9,11},{12,14},{13,15},{16,18},{17,... | collective-permute-start | bytes 1327112 | tf_op jit(solution)/shard_map/ppermute | solution.py:699
  228.9 32.2 %copy-start.13 = (f32[16,768]{1,0:T(8,128)S(1)}, f32[16,768]{1,0:T(8,128)}, u32[]{:S(2)}) copy-start(f32[16,768]{1,0:T(8,128)} %get-tuple-element.96) | copy-start | bytes 147460
  228.9 32.3 %copy-start.9 = (f32[16,1536]{1,0:T(8,128)S(1)}, f32[16,1536]{1,0:T(8,128)}, u32[]{:S(2)}) copy-start(f32[16,1536]{1,0:T(8,128)} %get-tuple-element.94) | copy-start | bytes 294916
  261.0 2.1 collective-permute-start.8
  261.4 14.8 %collective-permute-start.6 = (bf16[144,1536]{1,0:T(8,128)(2,1)S(1)}, bf16[144,1536]{1,0:T(8,128)(2,1)S(1)}, u32[]{:S(2)}, u32[]{:S(2)}) collective-permute-start(bf16[144,1536]{1,0:T(8,128)(2,1)S(1)} %get-tuple-element.120), channel_id=1, source_target_pairs={{2,0},{3,1},{6,4},{7,5},{10,8},{11,9},{14,12},{15,13},{18,16},{19,... | collective-permute-start | bytes 1327112 | tf_op jit(solution)/shard_map/ppermute | solution.py:699
  266.1 32.4 %collective-permute-start.9 = (bf16[144,1536]{1,0:T(8,128)(2,1)S(1)}, bf16[144,1536]{1,0:T(8,128)(2,1)S(1)}, u32[]{:S(2)}, u32[]{:S(2)}) collective-permute-start(bf16[144,1536]{1,0:T(8,128)(2,1)S(1)} %maximum_maximum_fusion.3), channel_id=1, source_target_pairs={{2,0},{3,1},{6,4},{7,5},{10,8},{11,9},{14,12},{15,13},{18,16},{19,... | collective-permute-start | bytes 1327112 | tf_op jit(solution)/shard_map/ppermute | solution.py:699
  277.3 21.1 %copy-start.8 = (f32[16,1536]{1,0:T(8,128)S(1)}, f32[16,1536]{1,0:T(8,128)}, u32[]{:S(2)}) copy-start(f32[16,1536]{1,0:T(8,128)} %get-tuple-element.95) | copy-start | bytes 294916
  296.9 24.0 %collective-permute-start.7 = (bf16[16,1792]{1,0:T(8,128)(2,1)}, bf16[16,1792]{1,0:T(8,128)(2,1)S(1)}, u32[]{:S(2)}, u32[]{:S(2)}) collective-permute-start(bf16[16,1792]{1,0:T(8,128)(2,1)} %get-tuple-element.76), channel_id=1, source_target_pairs={{1,0},{2,1},{3,2},{5,4},{6,5},{7,6},{9,8},{10,9},{11,10},{13,12},{... | collective-permute-start | bytes 172040 | tf_op jit(solution)/shard_map/ppermute | solution.py:699
  299.6 21.1 %copy-start.12 = (f32[16,768]{1,0:T(8,128)S(1)}, f32[16,768]{1,0:T(8,128)}, u32[]{:S(2)}) copy-start(f32[16,768]{1,0:T(8,128)} %get-tuple-element.97) | copy-start | bytes 147460
  319.2 17.6 %collective-permute-start.10 = (bf16[16,1792]{1,0:T(8,128)(2,1)}, bf16[16,1792]{1,0:T(8,128)(2,1)S(1)}, u32[]{:S(2)}, u32[]{:S(2)}) collective-permute-start(bf16[16,1792]{1,0:T(8,128)(2,1)} %get-tuple-element.88), channel_id=1, source_target_pairs={{1,0},{2,1},{3,2},{5,4},{6,5},{7,6},{9,8},{10,9},{11,10},{13,12},{... | collective-permute-start | bytes 172040 | tf_op jit(solution)/shard_map/ppermute | solution.py:699
  320.9 0.6 copy-start.10
  336.8 0.6 copy-start.11
  350.8 6.5 %copy-start.23 = (u32[32]{0:T(128)S(1)}, u32[32]{0:T(128)}, u32[]{:S(2)}) copy-start(u32[32]{0:T(128)} %constant.80) | copy-start | bytes 388
  350.8 7.7 %copy-start.15 = (s32[2]{0:T(128)S(1)}, s32[2]{0:T(128)}, u32[]{:S(2)}) copy-start(s32[2]{0:T(128)} %ids.13) | copy-start | bytes 28
  353.8 16.9 %all-to-all-start = ((bf16[8,2,16,768]{3,2,1,0:T(8,128)(2,1)}), bf16[8,2,16,768]{3,2,1,0:T(8,128)(2,1)S(1)}, u32[]{:S(2)}, u32[]{:S(2)}) async-start(bf16[8,2,16,768]{3,2,1,0:T(8,128)(2,1)} %pad_maximum_fusion.2), calls=%async_computation | async-start | bytes 786432 | tf_op jit(solution)/shard_map/all_to_all | solution.py:820
  357.2 19.9 %copy-start.2 = (bf16[512,768]{1,0:T(8,128)(2,1)S(1)}, bf16[512,768]{1,0:T(8,128)(2,1)}, u32[]{:S(2)}) copy-start(bf16[512,768]{1,0:T(8,128)(2,1)} %get-tuple-element.60) | copy-start | bytes 2359300
  357.2 19.9 %copy-start.3 = (bf16[512,768]{1,0:T(8,128)(2,1)S(1)}, bf16[512,768]{1,0:T(8,128)(2,1)}, u32[]{:S(2)}) copy-start(bf16[512,768]{1,0:T(8,128)(2,1)} %get-tuple-element.65) | copy-start | bytes 2359300
  372.0 1.8 collective-permute-start.11
  373.8 4.6 %copy-start = (f32[512,768]{1,0:T(8,128)S(1)}, f32[512,768]{1,0:T(8,128)}, u32[]{:S(2)}) copy-start(f32[512,768]{1,0:T(8,128)} %get-tuple-element.77) | copy-start | bytes 4718596
  373.8 4.6 %copy-start.1 = (f32[512,768]{1,0:T(8,128)S(1)}, f32[512,768]{1,0:T(8,128)}, u32[]{:S(2)}) copy-start(f32[512,768]{1,0:T(8,128)} %get-tuple-element.89) | copy-start | bytes 4718596
  373.8 12.7 %collective-permute-start.12 = (f32[8,12288]{1,0:T(8,128)S(1)}, f32[8,12288]{1,0:T(8,128)S(1)}, u32[]{:S(2)}, u32[]{:S(2)}) collective-permute-start(f32[8,12288]{1,0:T(8,128)S(1)} %add.114), channel_id=1, source_target_pairs={{0,2},{1,3},{2,0},{3,1},{4,6},{5,7},{6,4},{7,5},{8,10},{9,11},{10,... | collective-permute-start | bytes 1179656 | tf_op jit(solution)/shard_map/ppermute | solution.py:703
Sparse Core Ops, SparseCore 0:
  10.8 61.0 all-gather.3
  74.1 50.7 all-gather.7
  127.0 50.6 all-gather.5
